TPU v7x, 32 devices: a whole 2x2x4 slice. The times are simulated.
32 devices in a mesh: pairs: 8 (over y, x, core), aux: 4 (over z).
Axes of the slice: x: 2, y: 2, z: 4, core: 2. Of those that a mesh axis runs over, the one named last changes fastest.
Arguments:
- pair_orbits: int32 [512, 2], P('pairs'), may hold values from 0 to 255
- pno_count: int32 [512], P('pairs'), may hold values from 64 to 128
- partner: int32 [512, 12], P('pairs', 'aux'), may hold values from -1 to 511, as said below
- couple_orbit: int32 [512, 12], P('pairs', 'aux'), may hold values from 0 to 255
- couple_side: int32 [512, 12], P('pairs', 'aux'), may hold values from 0 to 1
- occ_fock: float32 [256, 256], replicated, may hold values from -2 to 1, as said below
- fit_left: bfloat16 [512, 128, 2048], P('pairs', None, 'aux'), may hold values from -0.8984375 to 0.8984375
- fit_right: bfloat16 [512, 128, 2048], P('pairs', None, 'aux'), may hold values from -0.8984375 to 0.8984375
- pno_coef: bfloat16 [512, 256, 128], P('pairs'), may hold values from -0.375 to 0.375
- virt_fock: bfloat16 [512, 128, 128], P('pairs'), may hold values from -0.25 to 3, as said below
- amps_in: float32 [512, 128, 128], P('pairs', 'aux'), may hold values from -1.8 to 1.8
Outputs:
- amps_out: float32 [512, 128, 128], P('pairs', 'aux')
Inputs may be any that keep to these rules, and one draw needn't show every extreme that they name: partner[p, c] is -1 (no coupling) or a pair held by another index of pairs; couplings are mutual: if slot c of p names q then slot c of q names p. In each slot, the pairs of one index of pairs name pairs of one other index at most 2 times, and 2 is reached in every slot. `occ_fock`: symmetric; its diagonal lies between -2 and -0.3. `virt_fock`: symmetric in its last two dimensions; its diagonal lies between 0.5 and 3.
All inputs are finite; a program needn't handle non-finite values.
Results may differ from a plain program's by a relative error of at most 0.0019.
Values may be sent and summed in bfloat16 or wider, within the bound.
No kernel may reach another device: no remote copies, remote signals or barrier semaphores. Data moves between devices by JAX's collectives and lax.ppermute only.
A program may use at most 192 MiB of HBM per device.

v0:
```python
import functools

import jax
import jax.numpy as jnp
from jax import lax
from jax.experimental import pallas as pl
from jax.experimental.pallas import tpu as pltpu
from jax.sharding import PartitionSpec as P

MOST = 2
SPARE_BYTES = 3 * 1024 * 1024
WIDE_BYTES = 48 * 1024 * 1024

SMEM = pl.BlockSpec(memory_space=pltpu.SMEM)
VMEM = pl.BlockSpec(memory_space=pltpu.VMEM)
HBM = pl.BlockSpec(memory_space=pltpu.HBM)
FREE = pl.CostEstimate(flops=0, bytes_accessed=0, transcendentals=0)


def dot(left, right, over_left, over_right):
    return lax.dot_general(
        left, right, (((over_left,), (over_right,)), ((), ())), preferred_element_type=jnp.float32
    )


def params(*arrays):
    held = sum(array.size * array.dtype.itemsize for array in arrays)
    needed = held + held // 8 + SPARE_BYTES
    return pltpu.CompilerParams(vmem_limit_bytes=max(needed, WIDE_BYTES))


def pair_places(partner, pair_dev, dev_count, arrival):
    slots = partner.shape[1]
    owner = jnp.where(partner >= 0, partner // pair_dev, -1)
    own_id = jnp.broadcast_to(jnp.arange(pair_dev, dtype=jnp.int32)[:, None], partner.shape)
    far_key = (partner - owner * pair_dev) * pair_dev + own_id
    none = pair_dev * pair_dev
    devs = jnp.arange(dev_count, dtype=jnp.int32)[None, :, None]
    hit = owner[:, None, :] == devs

    def ranked(key):
        left = jnp.where(hit, key[:, None, :], none)
        found = []
        for _ in range(MOST):
            least = jnp.min(left, axis=0)
            found.append(least)
            left = jnp.where(left == least[None], none, left)
        return jnp.stack(found, axis=-1).reshape(-1)

    send = ranked(own_id)
    send = jnp.where(send < none, send, 0)
    if not arrival:
        return send
    read = ranked(far_key)
    return send, jnp.where(read < none, lax.rem(read, pair_dev), -1)


def pack_rows(send_ref, half_ref, out_ref, held, sems):
    chunk = held.shape[0] // sems.shape[0]

    def store(turn):
        at = pl.ds(pl.multiple_of(turn * chunk, chunk), chunk)
        return pltpu.make_async_copy(held.at[at], out_ref.at[at], sems.at[turn])

    def body(turn, carry):
        for item in range(chunk):
            place = turn * chunk + item
            held[place] = half_ref[send_ref[place]]
        store(turn).start()
        return carry

    def finish(turn, carry):
        store(turn).wait()
        return carry

    lax.fori_loop(0, sems.shape[0], body, 0)
    lax.fori_loop(0, sems.shape[0], finish, 0)


def start_kernel(
    place_ref, send_ref, count_ref, amps_ref, kept_ref, half_ref, out_ref, held, sems
):
    pairs, rows, width = amps_ref.shape
    row_id = lax.broadcasted_iota(jnp.int32, (rows, width), 0) + place_ref[1] * rows
    col_id = lax.broadcasted_iota(jnp.int32, (rows, width), 1)
    last = jnp.maximum(row_id, col_id)

    def body(pair, carry):
        kept = jnp.where(last < count_ref[pair], amps_ref[pair], 0.0)
        kept_ref[pair] = kept
        half_ref[pair] = kept.astype(jnp.bfloat16)
        return carry

    lax.fori_loop(0, pairs, body, 0, unroll=4)
    pack_rows(send_ref, half_ref, out_ref, held, sems)


def coef_kernel(slots, place_ref, send_ref, coef_ref, *rest):
    outs, (held, in_sems, out_sems) = rest[:-3], rest[-3:]
    per_dev = slots * MOST

    def fetch(turn, item):
        far = place_ref[0] ^ (turn + 1)
        pair = send_ref[far * per_dev + item]
        place = turn * per_dev + item
        return pltpu.make_async_copy(coef_ref.at[pair], held.at[place], in_sems.at[place])

    def store(turn):
        return pltpu.make_async_copy(
            held.at[pl.ds(turn * per_dev, per_dev)], outs[turn], out_sems.at[turn]
        )

    for turn in range(len(outs)):
        for item in range(per_dev):
            fetch(turn, item).start()
    for turn in range(len(outs)):
        for item in range(per_dev):
            fetch(turn, item).wait()
        store(turn).start()
    for turn in range(len(outs)):
        store(turn).wait()


def put_rows(out_ref, pair, value):
    rows = out_ref.shape[2]
    for part in range(out_ref.shape[0]):
        out_ref[part, pair] = value[part * rows : (part + 1) * rows]


def element(matrix_ref, row, column):
    line = matrix_ref[pl.ds(row, 1), :]
    at = lax.broadcasted_iota(jnp.int32, line.shape, 1) == column
    return jnp.sum(jnp.where(at, line, 0.0), axis=1, keepdims=True)


def left_part(fock_rows, half_rows):
    return dot(fock_rows, half_rows, 0, 0)


def prepare_kernel(
    place_ref, count_ref, orbit_ref, occ_ref, left_ref, right_ref, fock_ref, kept_ref, half_ref,
    part_ref, scale_ref, own_ref, energy_ref,
):
    block, rows, width = kept_ref.shape
    first = pl.program_id(0) * block
    row_start = pl.multiple_of(place_ref[1] * rows, rows)
    row_id = lax.broadcasted_iota(jnp.int32, (rows, width), 0) + row_start
    col_id = lax.broadcasted_iota(jnp.int32, (rows, width), 1)
    last = jnp.maximum(row_id, col_id)
    eye_rows = row_id == col_id
    eye = lax.broadcasted_iota(jnp.int32, (width, width), 0) == lax.broadcasted_iota(
        jnp.int32, (width, width), 1
    )
    for pair in range(block):
        at = orbit_ref.shape[0] - 2 * (count_ref.shape[0] - first - pair)
        orbit, other = orbit_ref[at], orbit_ref[at + 1]
        energy = element(occ_ref, orbit, orbit) + element(occ_ref, other, other)
        energy_ref[pair] = jnp.broadcast_to(energy, (1, width))
        fock = fock_ref[pair]
        fock_rows = fock_ref[pair, pl.ds(row_start, rows), :]
        half = half_ref[pair]
        fitted = dot(left_ref[pair], right_ref[pair], 1, 1)
        put_rows(part_ref, pair, fitted + left_part(fock_rows, half))
        own_ref[pair] = dot(half, fock, 1, 0) - energy * kept_ref[pair]
        diag_cols = jnp.sum(jnp.where(eye, fock.astype(jnp.float32), 0.0), axis=0, keepdims=True)
        diag_rows = jnp.sum(
            jnp.where(eye_rows, fock_rows.astype(jnp.float32), 0.0), axis=1, keepdims=True
        )
        denominator = diag_rows + diag_cols - energy
        scale_ref[pair] = jnp.where(last < count_ref[first + pair], 1.0 / denominator, 0.0)


def any_live(read_ref, first, per_dev, rank):
    most = read_ref[first + rank]
    for item in range(rank + MOST, per_dev, MOST):
        most = jnp.maximum(most, read_ref[first + item])
    return most >= 0


def own_coef_kernel(slots, place_ref, read_ref, coef_ref, out_ref):
    per_dev = slots * MOST

    def body(turn, carry):
        far = place_ref[0] ^ (turn + 1)
        for item in range(per_dev):
            pair = jnp.maximum(read_ref[far * per_dev + item], 0)
            out_ref[turn * per_dev + item] = coef_ref[pair].T
        return carry

    lax.fori_loop(0, out_ref.shape[0] // per_dev, body, 0)


def projector_kernel(turns, place_ref, read_ref, own_ref, *rest):
    arrived, out_ref = rest[:-1], rest[-1]
    per_dev = arrived[0].shape[0]

    def rank_items(place, turn, rank):
        for item in range(rank, per_dev, MOST):
            own = own_ref[turn * per_dev + item]
            out_ref[place * per_dev + item] = dot(own, arrived[place][item], 1, 0).astype(
                jnp.bfloat16
            )

    for place, turn in enumerate(turns):
        far = place_ref[0] ^ (turn + 1)
        for rank in range(MOST):
            pl.when(any_live(read_ref, far * per_dev, per_dev, rank))(
                functools.partial(rank_items, place, turn, rank)
            )


def add_coupling(sets, place_ref, occ_ref, fetch, amps_ref, part_ref):
    parts, rows, width = part_ref.shape[0], part_ref.shape[2], part_ref.shape[3]
    per_dev = amps_ref.shape[2] // len(sets)
    slots = per_dev // MOST
    pairs = sets[0][1].shape[0] // (2 * slots + 2)
    side_at, pair_at = pairs * slots, 2 * pairs * slots

    def body(turn, place, proj_ref, read_ref, orbit_ref, offset):
        far = place_ref[0] ^ (turn + 1)
        if offset == 0:
            fetch(turn).wait()

        def rank_terms(rank):
            terms = []
            for item in range(rank, per_dev, MOST):
                pair = read_ref[far * per_dev + item]
                safe = jnp.maximum(pair, 0)
                entry = safe * slots + item // MOST
                orbit = orbit_ref[pair_at + 2 * safe + orbit_ref[side_at + entry]]
                coupled = element(occ_ref, orbit_ref[entry], orbit)
                weight = jnp.where(pair >= 0, -coupled, 0.0)
                proj = proj_ref[place * per_dev + item]
                amps = amps_ref[far, :, offset + item].reshape(width, width)
                mixed = dot(proj, amps, 1, 0).astype(jnp.bfloat16)
                terms.append((safe, weight * dot(mixed, proj, 1, 1)))
            for safe, term in terms:
                for part in range(parts):
                    part_ref[part, safe] += term[part * rows : (part + 1) * rows]

        for rank in range(MOST):
            pl.when(any_live(read_ref, far * per_dev, per_dev, rank))(
                functools.partial(rank_terms, rank)
            )

    for number, (read_ref, orbit_ref, groups) in enumerate(sets):
        for turns, proj_ref in groups:
            later = turns[min(1, len(turns) - 1)] - min(1, len(turns) - 1)

            def step(place, carry, first=turns[0], later=later, proj_ref=proj_ref):
                turn = jnp.where(place == 0, first, place + later)
                body(turn, place, proj_ref, read_ref, orbit_ref, number * per_dev)
                return carry

            lax.fori_loop(0, len(turns), step, 0)


def coupling_kernel(groups, scaled, place_ref, *refs):
    set_count = 1 if scaled else 2
    tables, refs = refs[: 2 * set_count], refs[2 * set_count :]
    occ_ref, early_ref, late_ref = refs[:3]
    sets = [(tables[0], tables[1], list(zip(groups, (early_ref, late_ref))))]
    if not scaled:
        every = tuple(range(sum(len(turns) for turns in groups)))
        sets.append((tables[2], tables[3], [(every, refs[3])]))
    amps_hbm, start_hbm, out_ref, extra_ref, amps_ref, amps_sems, start_sem, *rest = refs[
        2 + set_count :
    ]
    part_ref = out_ref if scaled else rest[0]
    parts, pairs, rows, width = start_hbm.shape
    given = amps_hbm.shape[1]
    first_row = (place_ref[1] // given) * given

    def fetch(turn):
        far = place_ref[0] ^ (turn + 1)
        return pltpu.make_async_copy(
            amps_hbm.at[far], amps_ref.at[far, pl.ds(first_row, given)], amps_sems.at[turn]
        )

    loads = [
        pltpu.make_async_copy(
            start_hbm.at[part], part_ref.at[part, pl.ds(0, pairs)], start_sem.at[part]
        )
        for part in range(parts)
    ]
    for load in loads:
        load.start()
    for turns in groups:
        for turn in turns:
            fetch(turn).start()
    if given < parts:
        blank = jnp.zeros(amps_ref.shape[2:], amps_ref.dtype)

        def clear(far, carry):
            for row in range(parts - given):
                amps_ref[far, lax.rem(first_row + given + row, parts)] = blank
            return carry

        lax.fori_loop(0, amps_ref.shape[0], clear, 0)
    for load in loads:
        load.wait()
    add_coupling(sets, place_ref, occ_ref, fetch, amps_ref, part_ref)
    if not scaled:

        def body(pair, carry):
            for part in range(parts):
                out_ref[part, pair] = part_ref[part, pair].astype(out_ref.dtype)
            extra_ref[pair] = part_ref[place_ref[1], pair]
            return carry

        lax.fori_loop(0, pairs, body, 0, unroll=4)
        return

    def body(pair, most):
        for part in range(parts):
            most = jnp.maximum(most, jnp.abs(part_ref[part, pair]))
        return most

    most = lax.fori_loop(0, pairs, body, jnp.zeros((rows, width), jnp.float32), unroll=4)
    most = jnp.max(jnp.max(most, axis=0, keepdims=True), axis=1, keepdims=True)
    power = jnp.maximum(jnp.ceil(jnp.log2(jnp.maximum(most, 1.0)) - 15.0), 0.0)
    for part in range(parts):
        out_ref[part, pairs] = jnp.broadcast_to(power * jnp.exp2(power), (rows, width))
    extra_ref[...] = jnp.broadcast_to(jnp.exp2(-power), (1, width))


def first_update_kernel(
    send_ref, sum_ref, own_ref, scale_ref, kept_ref, new_ref, half_ref, out_ref, held, sems
):
    def body(pair, carry):
        new = kept_ref[pair] - (sum_ref[pair] + own_ref[pair]) * scale_ref[pair]
        new_ref[pair] = new
        half_ref[pair] = new.astype(jnp.bfloat16)
        return carry

    lax.fori_loop(0, new_ref.shape[0], body, 0, unroll=4)
    pack_rows(send_ref, half_ref, out_ref, held, sems)


def between_kernel(
    place_ref, energy_ref, fock_ref, kept_ref, half_ref, before_ref, sum_ref, start_ref, old_ref,
    part_ref, own_ref,
):
    block, rows, width = kept_ref.shape
    row_start = pl.multiple_of(place_ref[1] * rows, rows)
    for pair in range(block):
        half = half_ref[pair]
        fock_rows = fock_ref[pair, pl.ds(row_start, rows), :]
        change = left_part(fock_rows, half) - left_part(fock_rows, before_ref[pair])
        for part in range(part_ref.shape[0]):
            part_ref[part, pair] = (
                start_ref[part, pair] - old_ref[part, pair] + change[part * rows : (part + 1) * rows]
            )
        own_ref[pair] = (
            dot(half, fock_ref[pair], 1, 0)
            - energy_ref[pair] * kept_ref[pair]
            + sum_ref[pair]
        )


def last_update_kernel(place_ref, got_ref, mine_ref, own_ref, scale_ref, kept_ref, new_ref):
    def body(pair, carry):
        total = mine_ref[pair]
        for turn in range(1, got_ref.shape[0]):
            part = lax.rem(place_ref[1] + turn, got_ref.shape[0])
            total = total + got_ref[part, pair].astype(jnp.float32)
        new_ref[pair] = kept_ref[pair] - (total + own_ref[pair]) * scale_ref[pair]
        return carry

    lax.fori_loop(0, new_ref.shape[0], body, 0, unroll=4)


def shape(dims, dtype):
    return jax.ShapeDtypeStruct(tuple(dims), dtype)


def per_device(
    pair_orbits,
    pno_count,
    partner,
    couple_orbit,
    couple_side,
    occ_fock,
    fit_left,
    fit_right,
    pno_coef,
    virt_fock,
    amps_in,
):
    pair_dev = pno_count.shape[0]
    width = virt_fock.shape[1]
    rows = amps_in.shape[1]
    slots = partner.shape[1]
    dev_count = lax.axis_size("pairs")
    aux_count = lax.axis_size("aux")
    all_slots = slots * aux_count
    per_dev = slots * MOST
    items = (dev_count - 1) * per_dev
    bf16, f32 = jnp.bfloat16, jnp.float32
    place = jnp.stack([lax.axis_index("pairs"), lax.axis_index("aux")]).astype(jnp.int32)

    orbits = [couple_orbit.reshape(-1), couple_side.reshape(-1), pair_orbits.reshape(-1)]
    orbits = jnp.concatenate(orbits)
    coef_send, coef_read = pair_places(partner, pair_dev, dev_count, True)

    def packed_coef(send):
        return pl.pallas_call(
            functools.partial(coef_kernel, slots),
            out_shape=tuple(
                shape((per_dev,) + pno_coef.shape[1:], bf16) for _ in range(dev_count - 1)
            ),
            in_specs=[SMEM, SMEM, HBM],
            out_specs=tuple(HBM for _ in range(dev_count - 1)),
            scratch_shapes=[
                pltpu.VMEM((items,) + pno_coef.shape[1:], bf16),
                pltpu.SemaphoreType.DMA((items,)),
                pltpu.SemaphoreType.DMA((dev_count - 1,)),
            ],
            compiler_params=params(shape((items,) + pno_coef.shape[1:], bf16)),
            cost_estimate=FREE,
            name="pack_coef",
        )(place, send, pno_coef)

    def sent_coef(coef_out):
        return [
            lax.ppermute(packed, "pairs", [(dev, dev ^ (turn + 1)) for dev in range(dev_count)])
            for turn, packed in enumerate(coef_out)
        ]

    coef_out = packed_coef(coef_send)
    tables = partner
    tables, coef_out = lax.optimization_barrier((tables, coef_out))
    coef_far = sent_coef(coef_out)
    half_count = aux_count // 2
    more = jnp.concatenate([tables, couple_orbit, couple_side], axis=1)
    shares = [tables]
    for turn in range(1, aux_count):
        turned = [(dev, (dev + turn) % aux_count) for dev in range(aux_count)]
        shares.append(lax.ppermute(more if turn == half_count else tables, "aux", turned))
    other = shares[half_count][:, slots:]
    shares[half_count] = shares[half_count][:, :slots]
    tables = jnp.zeros((aux_count,) + tables.shape, jnp.int32)
    owners = jnp.arange(aux_count)[:, None, None]
    for turn, share in enumerate(shares):
        owner = lax.rem(place[1] + aux_count - turn, aux_count)
        tables = jnp.where(owners == owner, share[None], tables)
    tables = tables.transpose(1, 0, 2).reshape(pair_dev, all_slots)
    send = pair_places(tables, pair_dev, dev_count, False)

    other_orbits = [other[:, :slots].reshape(-1), other[:, slots:].reshape(-1)]
    other_orbits = jnp.concatenate(other_orbits + [pair_orbits.reshape(-1)])
    other_send, other_read = pair_places(shares[half_count], pair_dev, dev_count, True)
    lower = [part for dev in range(half_count) for part in (dev, dev + half_count)]
    upper = [part for dev in range(half_count) for part in (dev + half_count, dev)]
    by_part = send.reshape(dev_count, aux_count, per_dev)
    half_send = jnp.where(
        place[1] < half_count,
        jnp.stack([by_part[:, part] for part in lower], axis=1),
        jnp.stack([by_part[:, part] for part in upper], axis=1),
    ).reshape(-1)

    places = dev_count * all_slots * MOST
    packed = shape((places, rows, width), bf16)
    pack_scratch = [pltpu.VMEM(packed.shape, bf16), pltpu.SemaphoreType.DMA((dev_count,))]
    kept, half, amps_out = pl.pallas_call(
        start_kernel,
        out_shape=(
            shape(amps_in.shape, f32),
            shape(amps_in.shape, bf16),
            packed,
        ),
        in_specs=[SMEM, SMEM, SMEM, VMEM],
        out_specs=(VMEM, VMEM, HBM),
        scratch_shapes=pack_scratch,
        compiler_params=params(amps_in, amps_in, amps_in, packed),
        cost_estimate=FREE,
        name="mask_and_pack",
    )(place, send, pno_count, amps_in)

    def exchange(packed):
        packed = packed.reshape(dev_count * aux_count, per_dev, rows, width)
        got = lax.all_to_all(packed, ("pairs", "aux"), split_axis=0, concat_axis=0, tiled=True)
        return got.reshape(dev_count, aux_count, per_dev, rows, width)

    ahead = slice(1, dev_count // 2 + 1)
    leading = slice(1, dev_count // 2 + 1, 2)
    amps_out, coef_far[leading] = lax.optimization_barrier((amps_out, coef_far[leading]))
    amps_far = exchange(amps_out)

    block = 8
    by_pair = lambda *dims: pl.BlockSpec((block,) + dims, lambda step: (step,) + (0,) * len(dims))
    fit = fit_left.shape[2]
    wide = by_pair(width, width)
    slab = by_pair(rows, width)
    line = by_pair(1, width)
    tall = pl.BlockSpec((aux_count, block, rows, width), lambda step: (0, step, 0, 0))
    by_rows = shape((aux_count, pair_dev, rows, width), f32)
    start, scale, mine, energy = pl.pallas_call(
        prepare_kernel,
        grid=(pair_dev // block,),
        out_shape=(
            by_rows,
            shape(amps_in.shape, f32),
            shape(amps_in.shape, f32),
            shape((pair_dev, 1, width), f32),
        ),
        in_specs=[SMEM, SMEM, SMEM, VMEM, by_pair(width, fit), by_pair(width, fit), wide, slab, slab],
        out_specs=(tall, slab, slab, line),
        compiler_params=pltpu.CompilerParams(vmem_limit_bytes=WIDE_BYTES),
        cost_estimate=FREE,
        name="integrals",
    )(place, pno_count, orbits, occ_fock, fit_left, fit_right, virt_fock, kept, half)

    own_shape = shape((items, width, pno_coef.shape[1]), bf16)

    def own_coef(read):
        return pl.pallas_call(
            functools.partial(own_coef_kernel, slots),
            out_shape=own_shape,
            in_specs=[SMEM, SMEM, VMEM],
            out_specs=VMEM,
            compiler_params=params(pno_coef, own_shape),
            name="own_coef",
        )(place, read, pno_coef)

    def projected(turns, read, own, arrived):
        out = shape((len(turns) * per_dev, width, width), bf16)
        return pl.pallas_call(
            functools.partial(projector_kernel, turns),
            out_shape=out,
            in_specs=[SMEM, SMEM] + [VMEM] * (1 + len(turns)),
            out_specs=VMEM,
            compiler_params=params(own, out, *arrived),
            name="projectors",
        )(place, read, own, *arrived)

    early = tuple(range(dev_count - 1)[ahead])
    groups = (early, tuple(turn for turn in range(dev_count - 1) if turn not in early))
    own = own_coef(coef_read)
    projectors = [
        projected(turns, coef_read, own, [coef_far[turn] for turn in turns]) for turns in groups
    ]

    def coupled(amps_far, start, tables, projectors, scaled):
        if scaled:
            out, extra = shape((aux_count, pair_dev + 1, rows, width), f32), shape((1, width), f32)
        else:
            out, extra = shape(start.shape, bf16), shape(amps_in.shape, f32)
        held = shape((dev_count, aux_count) + amps_far.shape[2:], bf16)
        return pl.pallas_call(
            functools.partial(coupling_kernel, groups, scaled),
            out_shape=(out, extra),
            in_specs=[SMEM] * (1 + len(tables)) + [VMEM] * (1 + len(projectors)) + [HBM] * 2,
            out_specs=(VMEM, VMEM),
            scratch_shapes=[
                pltpu.VMEM(held.shape, bf16),
                pltpu.SemaphoreType.DMA((dev_count - 1,)),
                pltpu.SemaphoreType.DMA((aux_count,)),
            ]
            + ([] if scaled else [pltpu.VMEM(start.shape, f32)]),
            compiler_params=params(out, amps_in, start, held, *projectors),
            name="coupling",
        )(place, *tables, occ_fock, *projectors, amps_far, start)

    tables = [coef_read, orbits]
    total, shrink = coupled(amps_far, start, tables, projectors, True)
    to_sum = (total * shrink).astype(jnp.float16)
    to_sum, other_send = lax.optimization_barrier((to_sum, other_send))
    other_out = list(packed_coef(other_send))
    other_far = [None] * len(other_out)

    def send_turns(turns):
        for turn in turns:
            pairs = [(dev, dev ^ (turn + 1)) for dev in range(dev_count)]
            other_far[turn] = lax.ppermute(other_out[turn], "pairs", pairs)

    first, second = groups
    send_turns(first)
    tied = ([other_out[turn] for turn in second], [other_far[turn] for turn in first])
    waiting, arrived = lax.optimization_barrier(tied)
    for turn, packed_turn in zip(second, waiting):
        other_out[turn] = packed_turn
    for turn, arrived_turn in zip(first, arrived):
        other_far[turn] = arrived_turn
    send_turns(second)
    got = lax.all_to_all(to_sum, "aux", split_axis=0, concat_axis=0, tiled=True)
    foreign = (jnp.arange(aux_count) != place[1])[:, None, None, None]
    grow = jnp.where(foreign, jnp.exp2(got[:, pair_dev:, :1].astype(f32)), 0.0)
    sums = lax.dynamic_index_in_dim(total, place[1], 0, keepdims=False)[:pair_dev]
    for turn in range(aux_count):
        sums = sums + got[turn, :pair_dev].astype(f32) * grow[turn]

    every = tuple(range(dev_count - 1))
    sums, other_far = lax.optimization_barrier((sums, other_far))
    other_projectors = projected(every, other_read, own_coef(other_read), other_far)

    before = half
    kept, half, amps_out = pl.pallas_call(
        first_update_kernel,
        out_shape=(
            shape(amps_in.shape, f32),
            shape(amps_in.shape, bf16),
            packed,
        ),
        in_specs=[SMEM] + [VMEM] * 4,
        out_specs=(VMEM, VMEM, HBM),
        scratch_shapes=pack_scratch,
        compiler_params=params(amps_in, amps_in, amps_in, amps_in, amps_in, amps_in, packed),
        name="first_update",
    )(half_send, sums, mine, scale, kept)

    halves = [
        [dev * aux_count + part for dev in range(dev_count) for part in range(first, last)]
        for first, last in ((0, half_count), (half_count, aux_count))
    ]
    amps_far = amps_out.reshape(dev_count * half_count, 2 * per_dev, rows, width)
    amps_far = lax.all_to_all(
        amps_far, ("pairs", "aux"), split_axis=0, concat_axis=0, axis_index_groups=halves, tiled=True
    ).reshape(dev_count, half_count, 2 * per_dev, rows, width)

    start, own = pl.pallas_call(
        between_kernel,
        grid=(pair_dev // block,),
        out_shape=(by_rows, shape(amps_in.shape, f32)),
        in_specs=[SMEM, line, wide, slab, slab, slab, slab, tall, tall],
        out_specs=(tall, slab),
        compiler_params=params(*[shape((2 * block,) + dims, f32) for dims in ((width, 3 * width), (rows, 6 * width))]),
        cost_estimate=pl.CostEstimate(
            flops=6 * pair_dev * width * width * rows,
            bytes_accessed=pair_dev * width * width * 10,
            transcendentals=0,
        ),
        name="between",
    )(place, energy, virt_fock, kept, half, before, sums, start, total)

    tables += [other_read, other_orbits]
    projectors.append(other_projectors)
    to_sum, mine = coupled(amps_far, start, tables, projectors, False)
    got = lax.all_to_all(to_sum, "aux", split_axis=0, concat_axis=0, tiled=True)

    return pl.pallas_call(
        last_update_kernel,
        out_shape=shape(amps_in.shape, f32),
        in_specs=[SMEM] + [VMEM] * 5,
        out_specs=VMEM,
        compiler_params=params(got, mine, own, scale, kept, amps_in),
        name="last_update",
    )(place, got, mine, own, scale, kept)


def solution(mesh):
    return jax.shard_map(
        per_device,
        mesh=mesh,
        in_specs=(
            P("pairs", None),
            P("pairs"),
            P("pairs", "aux"),
            P("pairs", "aux"),
            P("pairs", "aux"),
            P(),
            P("pairs", None, "aux"),
            P("pairs", None, "aux"),
            P("pairs", None, None),
            P("pairs", None, None),
            P("pairs", "aux", None),
        ),
        out_specs=P("pairs", "aux", None),
        check_vma=False,
    )
```

profile of v0, /device:TPU:0, one launch (start us, length us, event | category | flops | bytes accessed | tf_op | source)
XLA Modules:
  0.0 246.4 jit_solution(4933436522399756382)
XLA Ops:
  1.5 5.9 %pack_coef.2 = (bf16[6,256,128]{2,1,0:T(8,128)(2,1)}, bf16[6,256,128]{2,1,0:T(8,128)(2,1)S(1)}, bf16[6,256,128]{2,1,0:T(8,128)(2,1)}, bf16[6,256,128]{2,1,0:T(8,...) custom-call(s32[2]{0:T(128)S(1)} %pad_add_fusion.8.place_ref, ...), custom_call_target="tpu_custom_call" | custom-call | tf_op jit(solution)/shard_map/pack_coef/pallas_call | solution.py:407
  7.4 5.1 %collective-permute-start.1 = (s32[64,3]{0,1:T(4,128)S(1)}, s32[64,3]{0,1:T(4,128)S(1)}, u32[]{:S(2)}, u32[]{:S(2)}) collective-permute-start(s32[64,3]{0,1:T(4,128)S(1)} %copy-done.48), channel_id=1, source_target_pairs={{0,3},{1,0},{2,1},{3,2},{4,7},{5,4},{6,5},{7,6},{8,11},{9,8},{10,9... | collective-permute-start | bytes 2312 | tf_op jit(solution)/shard_map/ppermute | solution.py:439
  12.5 1.1 collective-permute-start
  14.3 1.9 collective-permute-start.4
  16.9 1.0 collective-permute-done.2
  19.7 2.1 mask_and_pack.1
  21.8 1.0 copy-done.7
  23.2 1.5 collective-permute-done.4.rest_2_
  24.6 4.9 %all-to-all-start = ((bf16[32,6,32,128]{3,2,1,0:T(8,128)(2,1)}), bf16[32,6,32,128]{3,2,1,0:T(8,128)(2,1)}, u32[]{:S(2)}, u32[]{:S(2)}) async-start(bf16[32,6,32,128]{3,2,1,0:T(8,128)(2,1)} %bitcast.10), calls=%async_computation | async-start | bytes 3145728 | tf_op jit(solution)/shard_map/all_to_all | solution.py:482
  29.5 1.5 collective-permute-start.5
  31.1 1.4 collective-permute-start.6
  33.0 2.3 collective-permute-start.9
  35.8 0.7 reshape.208
  37.2 0.7 reshape.206
  37.9 3.4 %own_coef.2.own_ref = bf16[42,128,256]{2,1,0:T(8,128)(2,1)S(1)} custom-call(s32[2]{0:T(128)S(1)} %pad_add_fusion.8.place_ref, s32[48]{0:T(128)S(1)} %compare_select_fusion.14.read_ref.refs_0_, bf16[64,256,128]{2,1,0:T(8,128)(2,1)} %coef_ref.7), custom_call_target="tpu_custom_call" | custom-call | tf_op jit(solution)/shard_map/own_coef/pallas_call | solution.py:517
  41.3 1.4 copy.57
  42.6 1.5 reshape.212
  44.8 1.4 reshape.211
  46.3 0.8 fusion.10
  47.1 1.5 fusion.9
  49.3 1.4 reshape.216
  50.7 0.8 pad_add_fusion.6
  51.4 1.6 copy-done.1
  53.0 1.2 copy-done.8
  54.9 12.4 %integrals.1 = (f32[4,64,32,128]{3,2,1,0:T(8,128)}, f32[64,32,128]{2,1,0:T(8,128)S(1)}, f32[64,32,128]{2,1,0:T(8,128)S(1)}, f32[64,1,128]{2,1,0:T(1,128)S(1)}) custom-call(s32[2]{0:T(128)S(1)} %pad_add_fusion.8.place_ref, s32[64]{0:T(128)S(1)} %copy-done.41, s32[512]{0:T(512)S(1)} %get-tuple-element.145.orbit_ref.refs_1_, f32[256,256]{1,0:T(8,128)S(1)} %copy-done.16, ...), custom_call_target="tpu_custom_call" | custom-call | tf_op jit(solution)/shard_map/integrals/pallas_call | solution.py:498
  68.6 7.5 %collective-permute-done.9.rest_2_ = bf16[6,256,128]{2,1,0:T(8,128)(2,1)} collective-permute-done((bf16[6,256,128]{2,1,0:T(8,128)(2,1)}, bf16[6,256,128]{2,1,0:T(8,128)(2,1)}, u32[]{:S(2)}, u32[]{:S(2)}) %collective-permute-start.9) | collective-permute-done | bytes 393248 | tf_op jit(solution)/shard_map/ppermute | solution.py:426
  76.1 1.3 projectors.4.refs_4_.refs_6_
  77.5 0.8 copy-done.4
  78.3 1.2 projectors.3.refs_3_.refs_5_
  79.6 1.1 copy-done.5
  80.6 0.9 copy-done.17
  81.6 5.8 %coupling.2 = (f32[4,65,32,128]{3,2,1,0:T(8,128)}, f32[1,128]{1,0:T(1,128)S(1)}) custom-call(s32[2]{0:T(128)S(1)} %pad_add_fusion.8.place_ref, s32[48]{0:T(128)S(1)} %compare_select_fusion.14.read_ref.refs_0_, s32[512]{0:T(512)S(1)} %get-tuple-element.145.orbit_ref.refs_1_, f32[256,256]{1,0:T(8,128)S(1)} %copy-done.17, ...), custom_call_target="tpu_custom_call" | custom-call | tf_op jit(solution)/shard_map/coupling/pallas_call | solution.py:550
  87.3 4.1 %multiply_convert_fusion = f16[4,65,32,128]{3,2,1,0:T(8,128)(2,1)} fusion(f32[4,65,32,128]{3,2,1,0:T(8,128)} %get-tuple-element.85.old_ref, f32[128]{0:T(128)S(1)} %bitcast.66), kind=kLoop, calls=%fused_computation | loop fusion | flops 2129920 | bytes 6390272 | tf_op jit(solution)/shard_map/convert_element_type | solution.py:567
  91.4 4.6 %all-to-all-start.1 = ((f16[4,65,32,128]{3,2,1,0:T(8,128)(2,1)}), f16[4,65,32,128]{3,2,1,0:T(8,128)(2,1)}, u32[]{:S(2)}, u32[]{:S(2)}) async-start(f16[4,65,32,128]{3,2,1,0:T(8,128)(2,1)} %multiply_convert_fusion), calls=%async_computation.1 | async-start | bytes 4259840 | tf_op jit(solution)/shard_map/all_to_all | solution.py:586
  96.2 5.4 %pack_coef.3 = (bf16[6,256,128]{2,1,0:T(8,128)(2,1)S(1)}, bf16[6,256,128]{2,1,0:T(8,128)(2,1)}, bf16[6,256,128]{2,1,0:T(8,128)(2,1)}, bf16[6,256,128]{2,1,0:T(8,...) custom-call(s32[2]{0:T(128)S(1)} %pad_add_fusion.8.place_ref, ...), custom_call_target="tpu_custom_call" | custom-call | tf_op jit(solution)/shard_map/pack_coef/pallas_call | solution.py:407
  101.6 4.2 %collective-permute-start.10 = (bf16[6,256,128]{2,1,0:T(8,128)(2,1)}, bf16[6,256,128]{2,1,0:T(8,128)(2,1)S(1)}, u32[]{:S(2)}, u32[]{:S(2)}) collective-permute-start(bf16[6,256,128]{2,1,0:T(8,128)(2,1)} %get-tuple-element.92), channel_id=1, source_target_pairs={{0,8},{4,12},{8,0},{12,4},{16,24},{20,28},{24,16},{28,20},{1,9},{5... | collective-permute-start | bytes 1179656 | tf_op jit(solution)/shard_map/ppermute | solution.py:575
  105.8 1.1 collective-permute-start.11
  108.1 7.4 %collective-permute-done.10.rest_1_ = bf16[6,256,128]{2,1,0:T(8,128)(2,1)S(1)} collective-permute-done((bf16[6,256,128]{2,1,0:T(8,128)(2,1)}, bf16[6,256,128]{2,1,0:T(8,128)(2,1)S(1)}, u32[]{:S(2)}, u32[]{:S(2)}) %collective-permute-start.10) | collective-permute-done | bytes 393248 | tf_op jit(solution)/shard_map/ppermute | solution.py:575
  115.6 8.8 %collective-permute-done.11.rest_2_ = bf16[6,256,128]{2,1,0:T(8,128)(2,1)S(1)} collective-permute-done((bf16[6,256,128]{2,1,0:T(8,128)(2,1)}, bf16[6,256,128]{2,1,0:T(8,128)(2,1)S(1)}, u32[]{:S(2)}, u32[]{:S(2)}) %collective-permute-start.11) | collective-permute-done | bytes 393248 | tf_op jit(solution)/shard_map/ppermute | solution.py:575
  124.4 0.7 copy-done.30
  125.1 0.7 copy-done.32
  126.4 1.8 collective-permute-start.15
  128.7 16.7 %all-to-all-done.1 = f16[4,65,32,128]{3,2,1,0:T(8,128)(2,1)} async-done(((f16[4,65,32,128]{3,2,1,0:T(8,128)(2,1)}), f16[4,65,32,128]{3,2,1,0:T(8,128)(2,1)}, u32[]{:S(2)}, u32[]{:S(2)}) %all-to-all-start.1) | async-done | bytes 2129952 | tf_op jit(solution)/shard_map/all_to_all | solution.py:586
  145.3 0.8 broadcast_select_fusion
  146.1 2.3 fusion.3.sum_ref
  148.4 1.2 copy-done.11
  149.6 1.2 copy-done.22
  150.8 2.2 first_update.1
  153.1 1.0 copy-done.13
  154.0 0.8 copy-done.26
  154.8 6.6 %all-to-all-start.2 = ((bf16[16,12,32,128]{3,2,1,0:T(8,128)(2,1)}), bf16[16,12,32,128]{3,2,1,0:T(8,128)(2,1)S(1)}, u32[]{:S(2)}, u32[]{:S(2)}) async-start(bf16[16,12,32,128]{3,2,1,0:T(8,128)(2,1)} %bitcast.67), calls=%async_computation.2 | async-start | bytes 3145728 | tf_op jit(solution)/shard_map/all_to_all | solution.py:617
  161.8 3.4 %own_coef.3.own_ref = bf16[42,128,256]{2,1,0:T(8,128)(2,1)S(1)} custom-call(s32[2]{0:T(128)S(1)} %pad_add_fusion.8.place_ref, s32[48]{0:T(128)S(1)} %compare_select_fusion.13.read_ref.refs_2_, bf16[64,256,128]{2,1,0:T(8,128)(2,1)} %coef_ref.7), custom_call_target="tpu_custom_call" | custom-call | tf_op jit(solution)/shard_map/own_coef/pallas_call | solution.py:517
  165.2 1.5 copy-done
  166.7 2.5 %projectors.5.refs_7_ = bf16[42,128,128]{2,1,0:T(8,128)(2,1)S(1)} custom-call(s32[2]{0:T(128)S(1)} %pad_add_fusion.8.place_ref, s32[48]{0:T(128)S(1)} %compare_select_fusion.13.read_ref.refs_2_, bf16[42,128,256]{2,1,0:T(8,128)(2,1)} %copy-done, bf16[6,256,128]{2,1,0:T(8,128)(2,1)} %collective-permute-done.14.rest_0_, bf16[6,256,128]{2,1,0:T(8,128)(2,1)S(1)} %copy-done.29, ...), custom_call_target="tpu_custom_call" | custom-call | tf_op jit(solution)/shard_map/projectors/pallas_call | solution.py:528
  169.3 1.1 copy-done.2
  170.3 9.1 %between.1 = (f32[4,64,32,128]{3,2,1,0:T(8,128)}, f32[64,32,128]{2,1,0:T(8,128)S(1)}) custom-call(s32[2]{0:T(128)S(1)} %pad_add_fusion.8.place_ref, f32[64,1,128]{2,1,0:T(1,128)S(1)} %copy-done.39, bf16[64,128,128]{2,1,0:T(8,128)(2,1)} %fock_ref.3, f32[64,32,128]{2,1,0:T(8,128)S(1)} %copy-done.14, bf16[64,32,128]{2,1,0:T(8,128)(2,1)S(1)} %copy-done.27, ...), custom_call_target="tpu_custom_call" | custom-call | flops 201326592 | bytes 10485760 | tf_op jit(solution)/shard_map/between/pallas_call | solution.py:621
  179.5 1.0 copy-done.24
  180.5 2.2 all-to-all-done.2
  182.7 1.3 copy-done.3
  184.0 1.1 copy-done.6
  185.1 0.9 copy-done.18
  186.0 4.9 %coupling.3 = (bf16[4,64,32,128]{3,2,1,0:T(8,128)(2,1)}, f32[64,32,128]{2,1,0:T(8,128)S(1)}) custom-call(s32[2]{0:T(128)S(1)} %pad_add_fusion.8.place_ref, s32[48]{0:T(128)S(1)} %compare_select_fusion.14.read_ref.refs_0_, s32[512]{0:T(512)S(1)} %get-tuple-element.145.orbit_ref.refs_1_, s32[48]{0:T(128)S(1)} %compare_select_fusion.13.read_ref.refs_2_, ...), custom_call_target="tpu_custom_call" | custom-call | tf_op jit(solution)/shard_map/coupling/pallas_call | solution.py:550
  191.0 52.3 %all_to_all.20.got_ref = bf16[4,64,32,128]{3,2,1,0:T(8,128)(2,1)} all-to-all(bf16[4,64,32,128]{3,2,1,0:T(8,128)(2,1)} %get-tuple-element.118), channel_id=1, replica_groups=mesh['pairs'=8,'aux'=4] {'aux'}, dimensions={0} | all-to-all | bytes 4194304 | tf_op jit(solution)/shard_map/all_to_all | solution.py:639
  243.3 3.1 %last_update.1 = f32[64,32,128]{2,1,0:T(8,128)} custom-call(s32[2]{0:T(128)S(1)} %pad_add_fusion.8.place_ref, bf16[4,64,32,128]{3,2,1,0:T(8,128)(2,1)} %all_to_all.20.got_ref, f32[64,32,128]{2,1,0:T(8,128)S(1)} %get-tuple-element.119.mine_ref, f32[64,32,128]{2,1,0:T(8,128)S(1)} %copy-done.25, f32[64,32,128]{2,1,0:T(8,128)S(1)} %copy-done.12, ...), custom_call_target="tpu_custom_call" | custom-call | tf_op jit(solution)/shard_map/last_update/pallas_call | solution.py:641
  (181 shorter events, 12.9 us)
Async XLA Ops:
  1.1 6.3 %copy-start.48 = (s32[64,3]{0,1:T(4,128)S(1)}, s32[64,3]{0,1:T(4,128)}, u32[]{:S(2)}) copy-start(s32[64,3]{0,1:T(4,128)} %param.13) | copy-start | bytes 2308
  1.1 11.4 %copy-start.51 = (s32[64,3]{0,1:T(4,128)S(1)}, s32[64,3]{0,1:T(4,128)}, u32[]{:S(2)}) copy-start(s32[64,3]{0,1:T(4,128)} %param.15) | copy-start | bytes 2308
  1.2 11.4 %copy-start.52 = (s32[64,3]{0,1:T(4,128)S(1)}, s32[64,3]{0,1:T(4,128)}, u32[]{:S(2)}) copy-start(s32[64,3]{0,1:T(4,128)} %param.14) | copy-start | bytes 2308
  1.5 18.2 %copy-start.23 = (f32[64,32,128]{2,1,0:T(8,128)S(1)}, f32[64,32,128]{2,1,0:T(8,128)}, u32[]{:S(2)}) copy-start(f32[64,32,128]{2,1,0:T(8,128)} %amps_ref.1) | copy-start | bytes 3145732
  1.5 18.2 %copy-start.40 = (s32[64]{0:T(128)S(1)}, s32[64]{0:T(128)}, u32[]{:S(2)}) copy-start(s32[64]{0:T(128)} %count_ref.3) | copy-start | bytes 772
  7.4 9.5 %collective-permute-start.1 = (s32[64,3]{0,1:T(4,128)S(1)}, s32[64,3]{0,1:T(4,128)S(1)}, u32[]{:S(2)}, u32[]{:S(2)}) collective-permute-start(s32[64,3]{0,1:T(4,128)S(1)} %copy-done.48), channel_id=1, source_target_pairs={{0,3},{1,0},{2,1},{3,2},{4,7},{5,4},{6,5},{7,6},{8,11},{9,8},{10,9... | collective-permute-start | bytes 2312 | tf_op jit(solution)/shard_map/ppermute | solution.py:439
  12.5 5.4 %collective-permute-start.2 = (s32[64,3]{0,1:T(4,128)S(1)}, s32[64,3]{0,1:T(4,128)S(1)}, u32[]{:S(2)}, u32[]{:S(2)}) collective-permute-start(s32[64,3]{0,1:T(4,128)S(1)} %copy-done.48), channel_id=1, source_target_pairs={{0,1},{1,2},{2,3},{3,0},{4,5},{5,6},{6,7},{7,4},{8,9},{9,10},{10,1... | collective-permute-start | bytes 2312 | tf_op jit(solution)/shard_map/ppermute | solution.py:439
  12.5 5.4 %collective-permute-start = (s32[64,9]{0,1:T(8,128)S(1)}, s32[64,9]{0,1:T(8,128)S(1)}, u32[]{:S(2)}, u32[]{:S(2)}) collective-permute-start(s32[64,9]{0,1:T(8,128)S(1)} %pad_add_fusion), channel_id=1, source_target_pairs={{0,2},{1,3},{2,0},{3,1},{4,6},{5,7},{6,4},{7,5},{8,10},{9,11},{10,... | collective-permute-start | bytes 6920 | tf_op jit(solution)/shard_map/ppermute | solution.py:439
  13.6 9.6 %collective-permute-start.3 = (bf16[6,256,128]{2,1,0:T(8,128)(2,1)S(1)}, bf16[6,256,128]{2,1,0:T(8,128)(2,1)S(1)}, u32[]{:S(2)}, u32[]{:S(2)}) collective-permute-start(bf16[6,256,128]{2,1,0:T(8,128)(2,1)S(1)} %get-tuple-element.72), channel_id=1, source_target_pairs={{0,8},{4,12},{8,0},{12,4},{16,24},{20,28},{24,16},{28,20},{1,9},{5... | collective-permute-start | bytes 1179656 | tf_op jit(solution)/shard_map/ppermute | solution.py:426
  14.3 10.3 %collective-permute-start.4 = (bf16[6,256,128]{2,1,0:T(8,128)(2,1)S(1)}, bf16[6,256,128]{2,1,0:T(8,128)(2,1)S(1)}, u32[]{:S(2)}, u32[]{:S(2)}) collective-permute-start(bf16[6,256,128]{2,1,0:T(8,128)(2,1)S(1)} %get-tuple-element.73), channel_id=1, source_target_pairs={{0,16},{4,20},{8,24},{12,28},{16,0},{20,4},{24,8},{28,12},{1,17},{... | collective-permute-start | bytes 1179656 | tf_op jit(solution)/shard_map/ppermute | solution.py:426
  19.4 5.2 %copy-start.46 = (s32[8,12,2]{1,0,2:T(8,128)}, s32[8,12,2]{1,0,2:T(8,128)S(1)}, u32[]{:S(2)}) copy-start(s32[8,12,2]{1,0,2:T(8,128)S(1)} %pad_add_fusion.1) | copy-start | bytes 2308
  19.7 15.9 %copy-start.55 = (s32[64,2]{0,1:T(2,128)S(1)}, s32[64,2]{0,1:T(2,128)}, u32[]{:S(2)}) copy-start(s32[64,2]{0,1:T(2,128)} %param.11) | copy-start | bytes 1540
  22.8 28.6 %copy-start.19 = (bf16[64,32,128]{2,1,0:T(8,128)(2,1)}, bf16[64,32,128]{2,1,0:T(8,128)(2,1)S(1)}, u32[]{:S(2)}) copy-start(bf16[64,32,128]{2,1,0:T(8,128)(2,1)S(1)} %get-tuple-element.83.half_ref.before_ref) | copy-start | bytes 1572868
  23.2 14.7 %copy-start.34 = (bf16[6,256,128]{2,1,0:T(8,128)(2,1)}, bf16[6,256,128]{2,1,0:T(8,128)(2,1)S(1)}, u32[]{:S(2)}) copy-start(bf16[6,256,128]{2,1,0:T(8,128)(2,1)S(1)} %collective-permute-done.3.rest_0_) | copy-start | bytes 1179652
  24.6 13.2 %copy-start.36 = (bf16[6,256,128]{2,1,0:T(8,128)(2,1)}, bf16[6,256,128]{2,1,0:T(8,128)(2,1)S(1)}, u32[]{:S(2)}) copy-start(bf16[6,256,128]{2,1,0:T(8,128)(2,1)S(1)} %collective-permute-done.4.rest_2_) | copy-start | bytes 1179652
  24.6 54.9 %all-to-all-start = ((bf16[32,6,32,128]{3,2,1,0:T(8,128)(2,1)}), bf16[32,6,32,128]{3,2,1,0:T(8,128)(2,1)}, u32[]{:S(2)}, u32[]{:S(2)}) async-start(bf16[32,6,32,128]{3,2,1,0:T(8,128)(2,1)} %bitcast.10), calls=%async_computation | async-start | bytes 3145728 | tf_op jit(solution)/shard_map/all_to_all | solution.py:482
  29.5 48.8 %collective-permute-start.5 = (bf16[6,256,128]{2,1,0:T(8,128)(2,1)}, bf16[6,256,128]{2,1,0:T(8,128)(2,1)}, u32[]{:S(2)}, u32[]{:S(2)}) collective-permute-start(bf16[6,256,128]{2,1,0:T(8,128)(2,1)} %get-tuple-element.75), channel_id=1, source_target_pairs={{0,12},{4,8},{8,4},{12,0},{16,28},{20,24},{24,20},{28,16},{1,13},{... | collective-permute-start | bytes 1179656 | tf_op jit(solution)/shard_map/ppermute | solution.py:426
  31.1 47.2 %collective-permute-start.6 = (bf16[6,256,128]{2,1,0:T(8,128)(2,1)}, bf16[6,256,128]{2,1,0:T(8,128)(2,1)}, u32[]{:S(2)}, u32[]{:S(2)}) collective-permute-start(bf16[6,256,128]{2,1,0:T(8,128)(2,1)} %get-tuple-element.77), channel_id=1, source_target_pairs={{0,20},{4,16},{8,28},{12,24},{16,4},{20,0},{24,12},{28,8},{1,21},{... | collective-permute-start | bytes 1179656 | tf_op jit(solution)/shard_map/ppermute | solution.py:426
  32.5 35.5 %collective-permute-start.7 = (bf16[6,256,128]{2,1,0:T(8,128)(2,1)}, bf16[6,256,128]{2,1,0:T(8,128)(2,1)}, u32[]{:S(2)}, u32[]{:S(2)}) collective-permute-start(bf16[6,256,128]{2,1,0:T(8,128)(2,1)} %get-tuple-element.78), channel_id=1, source_target_pairs={{0,4},{4,0},{8,12},{12,8},{16,20},{20,16},{24,28},{28,24},{1,5},{5... | collective-permute-start | bytes 1179656 | tf_op jit(solution)/shard_map/ppermute | solution.py:426
  32.6 36.0 %collective-permute-start.8 = (bf16[6,256,128]{2,1,0:T(8,128)(2,1)}, bf16[6,256,128]{2,1,0:T(8,128)(2,1)}, u32[]{:S(2)}, u32[]{:S(2)}) collective-permute-start(bf16[6,256,128]{2,1,0:T(8,128)(2,1)} %get-tuple-element.79), channel_id=1, source_target_pairs={{0,24},{4,28},{8,16},{12,20},{16,8},{20,12},{24,0},{28,4},{1,25},{... | collective-permute-start | bytes 1179656 | tf_op jit(solution)/shard_map/ppermute | solution.py:426
  33.0 43.1 %collective-permute-start.9 = (bf16[6,256,128]{2,1,0:T(8,128)(2,1)}, bf16[6,256,128]{2,1,0:T(8,128)(2,1)}, u32[]{:S(2)}, u32[]{:S(2)}) collective-permute-start(bf16[6,256,128]{2,1,0:T(8,128)(2,1)} %get-tuple-element.80), channel_id=1, source_target_pairs={{0,28},{4,24},{8,20},{12,16},{16,12},{20,8},{24,4},{28,0},{1,29},{... | collective-permute-start | bytes 1179656 | tf_op jit(solution)/shard_map/ppermute | solution.py:426
  37.9 6.2 %copy-start.54 = (s32[64,3]{0,1:T(4,128)S(1)}, s32[64,3]{0,1:T(4,128)}, u32[]{:S(2)}) copy-start(s32[64,3]{0,1:T(4,128)} %get-tuple-element.138) | copy-start | bytes 2308
  37.9 13.5 %copy-start.16 = (f32[256,256]{1,0:T(8,128)S(1)}, f32[256,256]{1,0:T(8,128)}, u32[]{:S(2)}) copy-start(f32[256,256]{1,0:T(8,128)} %refs_4_.1) | copy-start | bytes 786436
  47.1 2.2 copy-start.49
  51.4 1.6 copy-start.1
  53.0 1.2 copy-start.8
  54.9 12.4 %copy-start.56 = (s32[48]{0:T(128)S(1)}, s32[48]{0:T(128)}, u32[]{:S(2)}) copy-start(s32[48]{0:T(128)} %reshape.216) | copy-start | bytes 580
  67.3 10.1 %copy-start.10 = (f32[64,32,128]{2,1,0:T(8,128)}, f32[64,32,128]{2,1,0:T(8,128)S(1)}, u32[]{:S(2)}) copy-start(f32[64,32,128]{2,1,0:T(8,128)S(1)} %get-tuple-element.112.scale_ref) | copy-start | bytes 3145732
  67.3 10.1 %copy-start.21 = (f32[64,32,128]{2,1,0:T(8,128)}, f32[64,32,128]{2,1,0:T(8,128)S(1)}, u32[]{:S(2)}) copy-start(f32[64,32,128]{2,1,0:T(8,128)S(1)} %get-tuple-element.111.own_ref) | copy-start | bytes 3145732
  67.3 10.1 %copy-start.38 = (f32[64,1,128]{2,1,0:T(1,128)}, f32[64,1,128]{2,1,0:T(1,128)S(1)}, u32[]{:S(2)}) copy-start(f32[64,1,128]{2,1,0:T(1,128)S(1)} %get-tuple-element.114.energy_ref) | copy-start | bytes 98308
  68.0 10.3 %copy-start.35 = (bf16[6,256,128]{2,1,0:T(8,128)(2,1)S(1)}, bf16[6,256,128]{2,1,0:T(8,128)(2,1)}, u32[]{:S(2)}) copy-start(bf16[6,256,128]{2,1,0:T(8,128)(2,1)} %copy-done.34) | copy-start | bytes 1179652
  68.0 10.3 %copy-start.37 = (bf16[6,256,128]{2,1,0:T(8,128)(2,1)S(1)}, bf16[6,256,128]{2,1,0:T(8,128)(2,1)}, u32[]{:S(2)}) copy-start(bf16[6,256,128]{2,1,0:T(8,128)(2,1)} %copy-done.36) | copy-start | bytes 1179652
  91.4 4.6 %copy-start.47 = (s32[8,12,2]{1,0,2:T(8,128)S(1)}, s32[8,12,2]{1,0,2:T(8,128)}, u32[]{:S(2)}) copy-start(s32[8,12,2]{1,0,2:T(8,128)} %copy-done.46) | copy-start | bytes 2308
  91.4 4.7 %copy-start.42 = (s32[48]{0:T(128)S(1)}, s32[48]{0:T(128)}, u32[]{:S(2)}) copy-start(s32[48]{0:T(128)} %compare_select_fusion.7.send_ref) | copy-start | bytes 580
  91.4 53.9 %all-to-all-start.1 = ((f16[4,65,32,128]{3,2,1,0:T(8,128)(2,1)}), f16[4,65,32,128]{3,2,1,0:T(8,128)(2,1)}, u32[]{:S(2)}, u32[]{:S(2)}) async-start(f16[4,65,32,128]{3,2,1,0:T(8,128)(2,1)} %multiply_convert_fusion), calls=%async_computation.1 | async-start | bytes 4259840 | tf_op jit(solution)/shard_map/all_to_all | solution.py:586
  101.5 4.2 %copy-start.43 = (bf16[6,256,128]{2,1,0:T(8,128)(2,1)}, bf16[6,256,128]{2,1,0:T(8,128)(2,1)S(1)}, u32[]{:S(2)}) copy-start(bf16[6,256,128]{2,1,0:T(8,128)(2,1)S(1)} %get-tuple-element.102) | copy-start | bytes 1179652
  101.5 5.3 %copy-start.44 = (bf16[6,256,128]{2,1,0:T(8,128)(2,1)}, bf16[6,256,128]{2,1,0:T(8,128)(2,1)S(1)}, u32[]{:S(2)}) copy-start(bf16[6,256,128]{2,1,0:T(8,128)(2,1)S(1)} %get-tuple-element.101) | copy-start | bytes 1179652
  101.5 6.3 %copy-start.45 = (bf16[6,256,128]{2,1,0:T(8,128)(2,1)}, bf16[6,256,128]{2,1,0:T(8,128)(2,1)S(1)}, u32[]{:S(2)}) copy-start(bf16[6,256,128]{2,1,0:T(8,128)(2,1)S(1)} %get-tuple-element.96) | copy-start | bytes 1179652
  101.6 14.0 %collective-permute-start.10 = (bf16[6,256,128]{2,1,0:T(8,128)(2,1)}, bf16[6,256,128]{2,1,0:T(8,128)(2,1)S(1)}, u32[]{:S(2)}, u32[]{:S(2)}) collective-permute-start(bf16[6,256,128]{2,1,0:T(8,128)(2,1)} %get-tuple-element.92), channel_id=1, source_target_pairs={{0,8},{4,12},{8,0},{12,4},{16,24},{20,28},{24,16},{28,20},{1,9},{5... | collective-permute-start | bytes 1179656 | tf_op jit(solution)/shard_map/ppermute | solution.py:575
  105.8 18.6 %collective-permute-start.11 = (bf16[6,256,128]{2,1,0:T(8,128)(2,1)}, bf16[6,256,128]{2,1,0:T(8,128)(2,1)S(1)}, u32[]{:S(2)}, u32[]{:S(2)}) collective-permute-start(bf16[6,256,128]{2,1,0:T(8,128)(2,1)} %get-tuple-element.93), channel_id=1, source_target_pairs={{0,12},{4,8},{8,4},{12,0},{16,28},{20,24},{24,20},{28,16},{1,13},{... | collective-permute-start | bytes 1179656 | tf_op jit(solution)/shard_map/ppermute | solution.py:575
  106.9 18.2 %collective-permute-start.12 = (bf16[6,256,128]{2,1,0:T(8,128)(2,1)}, bf16[6,256,128]{2,1,0:T(8,128)(2,1)S(1)}, u32[]{:S(2)}, u32[]{:S(2)}) collective-permute-start(bf16[6,256,128]{2,1,0:T(8,128)(2,1)} %get-tuple-element.94), channel_id=1, source_target_pairs={{0,16},{4,20},{8,24},{12,28},{16,0},{20,4},{24,8},{28,12},{1,17},{... | collective-permute-start | bytes 1179656 | tf_op jit(solution)/shard_map/ppermute | solution.py:575
  107.3 18.6 %collective-permute-start.13 = (bf16[6,256,128]{2,1,0:T(8,128)(2,1)}, bf16[6,256,128]{2,1,0:T(8,128)(2,1)}, u32[]{:S(2)}, u32[]{:S(2)}) collective-permute-start(bf16[6,256,128]{2,1,0:T(8,128)(2,1)} %get-tuple-element.95), channel_id=1, source_target_pairs={{0,20},{4,16},{8,28},{12,24},{16,4},{20,0},{24,12},{28,8},{1,21},{... | collective-permute-start | bytes 1179656 | tf_op jit(solution)/shard_map/ppermute | solution.py:575
  107.9 40.5 %copy-start.9 = (f32[64,32,128]{2,1,0:T(8,128)S(1)}, f32[64,32,128]{2,1,0:T(8,128)}, u32[]{:S(2)}) copy-start(f32[64,32,128]{2,1,0:T(8,128)} %copy-done.7) | copy-start | bytes 3145732
  115.6 32.8 %copy-start.28 = (bf16[6,256,128]{2,1,0:T(8,128)(2,1)}, bf16[6,256,128]{2,1,0:T(8,128)(2,1)S(1)}, u32[]{:S(2)}) copy-start(bf16[6,256,128]{2,1,0:T(8,128)(2,1)S(1)} %collective-permute-done.10.rest_1_) | copy-start | bytes 1179652
  125.9 22.5 %collective-permute-start.14 = (bf16[6,256,128]{2,1,0:T(8,128)(2,1)}, bf16[6,256,128]{2,1,0:T(8,128)(2,1)}, u32[]{:S(2)}, u32[]{:S(2)}) collective-permute-start(bf16[6,256,128]{2,1,0:T(8,128)(2,1)} %copy-done.45), channel_id=1, source_target_pairs={{0,4},{4,0},{8,12},{12,8},{16,20},{20,16},{24,28},{28,24},{1,5},{5... | collective-permute-start | bytes 1179656 | tf_op jit(solution)/shard_map/ppermute | solution.py:575
  126.4 21.9 %collective-permute-start.15 = (bf16[6,256,128]{2,1,0:T(8,128)(2,1)}, bf16[6,256,128]{2,1,0:T(8,128)(2,1)}, u32[]{:S(2)}, u32[]{:S(2)}) collective-permute-start(bf16[6,256,128]{2,1,0:T(8,128)(2,1)} %copy-done.44), channel_id=1, source_target_pairs={{0,24},{4,28},{8,16},{12,20},{16,8},{20,12},{24,0},{28,4},{1,25},{... | collective-permute-start | bytes 1179656 | tf_op jit(solution)/shard_map/ppermute | solution.py:575
  128.2 20.2 %collective-permute-start.16 = (bf16[6,256,128]{2,1,0:T(8,128)(2,1)}, bf16[6,256,128]{2,1,0:T(8,128)(2,1)}, u32[]{:S(2)}, u32[]{:S(2)}) collective-permute-start(bf16[6,256,128]{2,1,0:T(8,128)(2,1)} %copy-done.43), channel_id=1, source_target_pairs={{0,28},{4,24},{8,20},{12,16},{16,12},{20,8},{24,4},{28,0},{1,29},{... | collective-permute-start | bytes 1179656 | tf_op jit(solution)/shard_map/ppermute | solution.py:575
  148.4 1.2 copy-start.11
  149.6 1.2 copy-start.22
  154.8 6.6 %copy-start.50 = (s32[8,3]{0,1:T(4,128)S(1)}, s32[8,3]{0,1:T(4,128)}, u32[]{:S(2)}) copy-start(s32[8,3]{0,1:T(4,128)} %copy-done.49) | copy-start | bytes 292
  154.8 6.6 %copy-start.53 = (s32[8,3]{0,1:T(4,128)S(1)}, s32[8,3]{0,1:T(4,128)}, u32[]{:S(2)}) copy-start(s32[8,3]{0,1:T(4,128)} %get-tuple-element.122) | copy-start | bytes 292
  154.8 27.8 %all-to-all-start.2 = ((bf16[16,12,32,128]{3,2,1,0:T(8,128)(2,1)}), bf16[16,12,32,128]{3,2,1,0:T(8,128)(2,1)S(1)}, u32[]{:S(2)}, u32[]{:S(2)}) async-start(bf16[16,12,32,128]{3,2,1,0:T(8,128)(2,1)} %bitcast.67), calls=%async_computation.2 | async-start | bytes 3145728 | tf_op jit(solution)/shard_map/all_to_all | solution.py:617
  161.7 4.9 %copy-start.29 = (bf16[6,256,128]{2,1,0:T(8,128)(2,1)S(1)}, bf16[6,256,128]{2,1,0:T(8,128)(2,1)}, u32[]{:S(2)}) copy-start(bf16[6,256,128]{2,1,0:T(8,128)(2,1)} %copy-done.28) | copy-start | bytes 1179652
  161.7 4.9 %copy-start.31 = (bf16[6,256,128]{2,1,0:T(8,128)(2,1)S(1)}, bf16[6,256,128]{2,1,0:T(8,128)(2,1)}, u32[]{:S(2)}) copy-start(bf16[6,256,128]{2,1,0:T(8,128)(2,1)} %copy-done.30) | copy-start | bytes 1179652
  161.7 4.9 %copy-start.33 = (bf16[6,256,128]{2,1,0:T(8,128)(2,1)S(1)}, bf16[6,256,128]{2,1,0:T(8,128)(2,1)}, u32[]{:S(2)}) copy-start(bf16[6,256,128]{2,1,0:T(8,128)(2,1)} %copy-done.32) | copy-start | bytes 1179652
  165.2 1.5 copy-start
  166.7 3.7 %copy-start.14 = (f32[64,32,128]{2,1,0:T(8,128)S(1)}, f32[64,32,128]{2,1,0:T(8,128)}, u32[]{:S(2)}) copy-start(f32[64,32,128]{2,1,0:T(8,128)} %copy-done.13) | copy-start | bytes 3145732
  166.7 3.6 %copy-start.20 = (bf16[64,32,128]{2,1,0:T(8,128)(2,1)S(1)}, bf16[64,32,128]{2,1,0:T(8,128)(2,1)}, u32[]{:S(2)}) copy-start(bf16[64,32,128]{2,1,0:T(8,128)(2,1)} %copy-done.19) | copy-start | bytes 1572868
  166.7 3.6 %copy-start.27 = (bf16[64,32,128]{2,1,0:T(8,128)(2,1)S(1)}, bf16[64,32,128]{2,1,0:T(8,128)(2,1)}, u32[]{:S(2)}) copy-start(bf16[64,32,128]{2,1,0:T(8,128)(2,1)} %copy-done.26) | copy-start | bytes 1572868
  166.7 3.6 %copy-start.39 = (f32[64,1,128]{2,1,0:T(1,128)S(1)}, f32[64,1,128]{2,1,0:T(1,128)}, u32[]{:S(2)}) copy-start(f32[64,1,128]{2,1,0:T(1,128)} %copy-done.38) | copy-start | bytes 98308
  182.7 1.3 copy-start.3
  191.0 52.3 %copy-start.12 = (f32[64,32,128]{2,1,0:T(8,128)S(1)}, f32[64,32,128]{2,1,0:T(8,128)}, u32[]{:S(2)}) copy-start(f32[64,32,128]{2,1,0:T(8,128)} %copy-done.10) | copy-start | bytes 3145732
  191.0 52.3 %copy-start.15 = (f32[64,32,128]{2,1,0:T(8,128)S(1)}, f32[64,32,128]{2,1,0:T(8,128)}, u32[]{:S(2)}) copy-start(f32[64,32,128]{2,1,0:T(8,128)} %copy-done.13) | copy-start | bytes 3145732
  191.0 52.3 %copy-start.25 = (f32[64,32,128]{2,1,0:T(8,128)S(1)}, f32[64,32,128]{2,1,0:T(8,128)}, u32[]{:S(2)}) copy-start(f32[64,32,128]{2,1,0:T(8,128)} %copy-done.24) | copy-start | bytes 3145732
  (13 other events, 11.8 us)
where the time goes:
time: 251 us; the launch traced here: 246 us
  Pallas kernels  62.7 us (25%)
  blocking collectives  52.3 us (21%)
  waiting for transfers between devices  46 us (18%)
  starting transfers between devices  39.6 us (16%)
  local copies, waits for them, and re-layouts  31.5 us (13%)
  other arithmetic  13.4 us (5%)
    all_to_all x1, blocking collectives, per_device(): got = lax.all_to_all(to_sum, 'aux', split_axis=0, concat_axis=0, tiled=True)  52.3 us
    unnamed x117, local copies, waits for them, and re-layouts  20.3 us
    all_to_all x1, waiting for transfers between devices, per_device(): got = lax.all_to_all(to_sum, 'aux', split_axis=0, concat_axis=0, tiled=True)  16.7 us
    ppermute x7, waiting for transfers between devices, send_turns(): other_far[turn] = lax.ppermute(other_out[turn], 'pairs', pairs)  16.2 us
    pallas_call x1, Pallas kernels, per_device(): pl.pallas_call(prepare_kernel, grid=(pair_dev // block,), out_shape=(by_r...  12.4 us
    pallas_call x2, Pallas kernels, packed_coef(): pl.pallas_call(functools.partial(coef_kernel, slots), out_shape=tuple((sh...  11.3 us
    pallas_call x2, Pallas kernels, coupled(): pl.pallas_call(functools.partial(coupling_kernel, groups, scaled), out_sh...  10.7 us
    ppermute x7, waiting for transfers between devices, sent_coef(): lax.ppermute(packed, 'pairs', [(dev, dev ^ turn + 1) for dev in range(dev...  9.92 us
  transfers between devices with their start and end apart: 20, of which 9 were waited for; matrix products, arithmetic and copies ran while one was open for 8% of the time, Pallas kernels for 17%

commit v1 on v0

--- a/solution.py
+++ b/solution.py
@@ -429,7 +429,6 @@
 
     coef_out = packed_coef(coef_send)
     tables = partner
-    tables, coef_out = lax.optimization_barrier((tables, coef_out))
     coef_far = sent_coef(coef_out)
     half_count = aux_count // 2
     more = jnp.concatenate([tables, couple_orbit, couple_side], axis=1)

time: 251 us -> 254 us (1.012); the launches traced: 246 us -> 257 us
  Pallas kernels: 62.7 us -> 72.6 us
  starting transfers between devices: 39.6 us -> 34.7 us
  waiting for transfers between devices: 46 us -> 49.5 us
    pallas_call x2, Pallas kernels: 10.7 us -> 19.8 us  [coupled(): pl.pallas_call(functools.partial(coupling_kernel, groups, scaled), out_sh...]
    all_to_all x1, waiting for transfers between devices: 16.7 us -> 20.6 us  [per_device(): got = lax.all_to_all(to_sum, 'aux', split_axis=0, concat_axis=0, tiled=True)]
    pallas_call x3, Pallas kernels: 5.1 us -> 7.89 us  [projected(): pl.pallas_call(functools.partial(projector_kernel, turns), out_shape=out,...]
    all_to_all x1, starting transfers between devices: 6.61 us -> 3.84 us  [per_device(): lax.all_to_all(amps_far, ('pairs', 'aux'), split_axis=0, concat_axis=0, a...]
  transfers between devices with their start and end apart: 20 -> 20, of which waited for: 9 -> 8; matrix products, arithmetic and copies ran while one was open for 8% -> 8% of each run, Pallas kernels for 17% -> 18%
where the time goes in v1:
time: 254 us; the launch traced here: 257 us
  Pallas kernels  72.6 us (29%)
  blocking collectives  53.8 us (21%)
  waiting for transfers between devices  49.5 us (19%)
  starting transfers between devices  34.7 us (14%)
  local copies, waits for them, and re-layouts  31.5 us (12%)
  other arithmetic  14.2 us (6%)
    all_to_all x1, blocking collectives, per_device(): got = lax.all_to_all(to_sum, 'aux', split_axis=0, concat_axis=0, tiled=True)  53.8 us
    all_to_all x1, waiting for transfers between devices, per_device(): got = lax.all_to_all(to_sum, 'aux', split_axis=0, concat_axis=0, tiled=True)  20.6 us
    unnamed x117, local copies, waits for them, and re-layouts  20.3 us
    pallas_call x2, Pallas kernels, coupled(): pl.pallas_call(functools.partial(coupling_kernel, groups, scaled), out_sh...  19.8 us
    ppermute x7, waiting for transfers between devices, send_turns(): other_far[turn] = lax.ppermute(other_out[turn], 'pairs', pairs)  16.3 us
    pallas_call x1, Pallas kernels, per_device(): pl.pallas_call(prepare_kernel, grid=(pair_dev // block,), out_shape=(by_r...  12.4 us
    ppermute x7, waiting for transfers between devices, sent_coef(): lax.ppermute(packed, 'pairs', [(dev, dev ^ turn + 1) for dev in range(dev...  11.9 us
    pallas_call x1, Pallas kernels, per_device(): pl.pallas_call(between_kernel, grid=(pair_dev // block,), out_shape=(by_r...  9.13 us
  transfers between devices with their start and end apart: 20, of which 8 were waited for; matrix products, arithmetic and copies ran while one was open for 8% of the time, Pallas kernels for 18%

profile of v1, /device:TPU:0, one launch (start us, length us, event | category | flops | bytes accessed | tf_op | source)
XLA Modules:
  0.0 256.9 jit_solution(1969493463098668900)
XLA Ops:
  0.0 5.0 %collective-permute-start.1 = (s32[64,3]{0,1:T(4,128)}, s32[64,3]{0,1:T(4,128)S(1)}, u32[]{:S(2)}, u32[]{:S(2)}) collective-permute-start(s32[64,3]{0,1:T(4,128)} %param.13), channel_id=1, source_target_pairs={{0,3},{1,0},{2,1},{3,2},{4,7},{5,4},{6,5},{7,6},{8,11},{9,8},{10,9... | collective-permute-start | bytes 2312 | tf_op jit(solution)/shard_map/ppermute | solution.py:438
  5.1 0.8 pad_add_fusion
  5.8 1.0 collective-permute-start
  8.3 4.9 %pack_coef.2 = (bf16[6,256,128]{2,1,0:T(8,128)(2,1)}, bf16[6,256,128]{2,1,0:T(8,128)(2,1)S(1)}, bf16[6,256,128]{2,1,0:T(8,128)(2,1)}, bf16[6,256,128]{2,1,0:T(8,...) custom-call(s32[2]{0:T(128)S(1)} %pad_add_fusion.8.place_ref, ...), custom_call_target="tpu_custom_call" | custom-call | tf_op jit(solution)/shard_map/pack_coef/pallas_call | solution.py:407
  13.2 1.6 collective-permute-start.3
  14.9 0.9 collective-permute-start.4
  18.4 2.1 mask_and_pack.1
  20.5 1.0 copy-done.7
  21.5 1.5 collective-permute-done.3.rest_0_
  23.0 2.3 collective-permute-done.4.rest_2_
  25.3 5.0 %all-to-all-start = ((bf16[32,6,32,128]{3,2,1,0:T(8,128)(2,1)}), bf16[32,6,32,128]{3,2,1,0:T(8,128)(2,1)}, u32[]{:S(2)}, u32[]{:S(2)}) async-start(bf16[32,6,32,128]{3,2,1,0:T(8,128)(2,1)} %bitcast.10), calls=%async_computation | async-start | bytes 3145728 | tf_op jit(solution)/shard_map/all_to_all | solution.py:481
  30.3 1.5 collective-permute-start.5
  31.8 1.4 collective-permute-start.6
  33.8 2.3 collective-permute-start.9
  38.7 3.4 %own_coef.2.own_ref = bf16[42,128,256]{2,1,0:T(8,128)(2,1)S(1)} custom-call(s32[2]{0:T(128)S(1)} %pad_add_fusion.8.place_ref, s32[48]{0:T(128)S(1)} %compare_select_fusion.14.read_ref.refs_0_, bf16[64,256,128]{2,1,0:T(8,128)(2,1)} %coef_ref.7), custom_call_target="tpu_custom_call" | custom-call | tf_op jit(solution)/shard_map/own_coef/pallas_call | solution.py:516
  42.1 1.4 copy.56
  43.4 1.5 reshape.211
  45.6 1.4 reshape.210
  47.0 0.8 fusion.10
  47.9 1.5 fusion.9
  50.1 1.4 reshape.216
  51.4 0.8 pad_add_fusion.6
  52.2 1.6 copy-done.1
  53.8 1.2 copy-done.8
  55.7 12.4 %integrals.1 = (f32[4,64,32,128]{3,2,1,0:T(8,128)}, f32[64,32,128]{2,1,0:T(8,128)S(1)}, f32[64,32,128]{2,1,0:T(8,128)S(1)}, f32[64,1,128]{2,1,0:T(1,128)S(1)}) custom-call(s32[2]{0:T(128)S(1)} %pad_add_fusion.8.place_ref, s32[64]{0:T(128)S(1)} %copy-done.41, s32[512]{0:T(512)S(1)} %get-tuple-element.129.orbit_ref.refs_1_, f32[256,256]{1,0:T(8,128)S(1)} %copy-done.16, ...), custom_call_target="tpu_custom_call" | custom-call | tf_op jit(solution)/shard_map/integrals/pallas_call | solution.py:497
  69.4 7.5 %collective-permute-done.9.rest_2_ = bf16[6,256,128]{2,1,0:T(8,128)(2,1)} collective-permute-done((bf16[6,256,128]{2,1,0:T(8,128)(2,1)}, bf16[6,256,128]{2,1,0:T(8,128)(2,1)}, u32[]{:S(2)}, u32[]{:S(2)}) %collective-permute-start.9) | collective-permute-done | bytes 393248 | tf_op jit(solution)/shard_map/ppermute | solution.py:426
  76.9 1.9 projectors.4.refs_4_.refs_6_
  78.8 0.8 copy-done.4
  79.6 2.0 projectors.3.refs_3_.refs_5_
  81.7 1.1 copy-done.5
  82.7 0.9 copy-done.17
  83.7 8.8 %coupling.2 = (f32[4,65,32,128]{3,2,1,0:T(8,128)}, f32[1,128]{1,0:T(1,128)S(1)}) custom-call(s32[2]{0:T(128)S(1)} %pad_add_fusion.8.place_ref, s32[48]{0:T(128)S(1)} %compare_select_fusion.14.read_ref.refs_0_, s32[512]{0:T(512)S(1)} %get-tuple-element.129.orbit_ref.refs_1_, f32[256,256]{1,0:T(8,128)S(1)} %copy-done.17, ...), custom_call_target="tpu_custom_call" | custom-call | tf_op jit(solution)/shard_map/coupling/pallas_call | solution.py:549
  92.4 4.1 %multiply_convert_fusion = f16[4,65,32,128]{3,2,1,0:T(8,128)(2,1)} fusion(f32[4,65,32,128]{3,2,1,0:T(8,128)} %get-tuple-element.69.old_ref, f32[128]{0:T(128)S(1)} %bitcast.66), kind=kLoop, calls=%fused_computation | loop fusion | flops 2129920 | bytes 6390272 | tf_op jit(solution)/shard_map/convert_element_type | solution.py:566
  96.5 4.6 %all-to-all-start.1 = ((f16[4,65,32,128]{3,2,1,0:T(8,128)(2,1)}), f16[4,65,32,128]{3,2,1,0:T(8,128)(2,1)}, u32[]{:S(2)}, u32[]{:S(2)}) async-start(f16[4,65,32,128]{3,2,1,0:T(8,128)(2,1)} %multiply_convert_fusion), calls=%async_computation.1 | async-start | bytes 4259840 | tf_op jit(solution)/shard_map/all_to_all | solution.py:585
  101.3 4.2 %pack_coef.3 = (bf16[6,256,128]{2,1,0:T(8,128)(2,1)S(1)}, bf16[6,256,128]{2,1,0:T(8,128)(2,1)}, bf16[6,256,128]{2,1,0:T(8,128)(2,1)}, bf16[6,256,128]{2,1,0:T(8,...) custom-call(s32[2]{0:T(128)S(1)} %pad_add_fusion.8.place_ref, ...), custom_call_target="tpu_custom_call" | custom-call | tf_op jit(solution)/shard_map/pack_coef/pallas_call | solution.py:407
  105.5 2.0 collective-permute-start.10
  107.5 0.8 collective-permute-start.11
  108.5 1.2 collective-permute-start.13
  109.9 7.5 %collective-permute-done.10.rest_1_ = bf16[6,256,128]{2,1,0:T(8,128)(2,1)S(1)} collective-permute-done((bf16[6,256,128]{2,1,0:T(8,128)(2,1)}, bf16[6,256,128]{2,1,0:T(8,128)(2,1)S(1)}, u32[]{:S(2)}, u32[]{:S(2)}) %collective-permute-start.10) | collective-permute-done | bytes 393248 | tf_op jit(solution)/shard_map/ppermute | solution.py:574
  117.4 8.8 %collective-permute-done.11.rest_2_ = bf16[6,256,128]{2,1,0:T(8,128)(2,1)S(1)} collective-permute-done((bf16[6,256,128]{2,1,0:T(8,128)(2,1)}, bf16[6,256,128]{2,1,0:T(8,128)(2,1)S(1)}, u32[]{:S(2)}, u32[]{:S(2)}) %collective-permute-start.11) | collective-permute-done | bytes 393248 | tf_op jit(solution)/shard_map/ppermute | solution.py:574
  126.2 0.7 copy-done.30
  126.9 0.7 copy-done.32
  127.9 1.9 collective-permute-start.15
  130.4 20.6 %all-to-all-done.1 = f16[4,65,32,128]{3,2,1,0:T(8,128)(2,1)} async-done(((f16[4,65,32,128]{3,2,1,0:T(8,128)(2,1)}), f16[4,65,32,128]{3,2,1,0:T(8,128)(2,1)}, u32[]{:S(2)}, u32[]{:S(2)}) %all-to-all-start.1) | async-done | bytes 2129952 | tf_op jit(solution)/shard_map/all_to_all | solution.py:585
  151.1 0.8 broadcast_select_fusion
  151.8 2.3 fusion.3.sum_ref
  154.1 1.2 copy-done.11
  155.4 1.2 copy-done.22
  156.6 2.2 first_update.1
  158.8 1.0 copy-done.13
  159.8 0.8 copy-done.26
  160.6 3.8 %all-to-all-start.2 = ((bf16[16,12,32,128]{3,2,1,0:T(8,128)(2,1)}), bf16[16,12,32,128]{3,2,1,0:T(8,128)(2,1)S(1)}, u32[]{:S(2)}, u32[]{:S(2)}) async-start(bf16[16,12,32,128]{3,2,1,0:T(8,128)(2,1)} %bitcast.67), calls=%async_computation.2 | async-start | bytes 3145728 | tf_op jit(solution)/shard_map/all_to_all | solution.py:616
  164.7 3.4 %own_coef.3.own_ref = bf16[42,128,256]{2,1,0:T(8,128)(2,1)S(1)} custom-call(s32[2]{0:T(128)S(1)} %pad_add_fusion.8.place_ref, s32[48]{0:T(128)S(1)} %compare_select_fusion.13.read_ref.refs_2_, bf16[64,256,128]{2,1,0:T(8,128)(2,1)} %coef_ref.7), custom_call_target="tpu_custom_call" | custom-call | tf_op jit(solution)/shard_map/own_coef/pallas_call | solution.py:516
  168.1 1.5 copy-done
  169.7 4.0 %projectors.5.refs_7_ = bf16[42,128,128]{2,1,0:T(8,128)(2,1)S(1)} custom-call(s32[2]{0:T(128)S(1)} %pad_add_fusion.8.place_ref, s32[48]{0:T(128)S(1)} %compare_select_fusion.13.read_ref.refs_2_, bf16[42,128,256]{2,1,0:T(8,128)(2,1)} %copy-done, bf16[6,256,128]{2,1,0:T(8,128)(2,1)} %collective-permute-done.14.rest_0_, bf16[6,256,128]{2,1,0:T(8,128)(2,1)S(1)} %copy-done.29, ...), custom_call_target="tpu_custom_call" | custom-call | tf_op jit(solution)/shard_map/projectors/pallas_call | solution.py:527
  173.7 1.1 copy-done.2
  174.8 9.1 %between.1 = (f32[4,64,32,128]{3,2,1,0:T(8,128)}, f32[64,32,128]{2,1,0:T(8,128)S(1)}) custom-call(s32[2]{0:T(128)S(1)} %pad_add_fusion.8.place_ref, f32[64,1,128]{2,1,0:T(1,128)S(1)} %copy-done.39, bf16[64,128,128]{2,1,0:T(8,128)(2,1)} %fock_ref.3, f32[64,32,128]{2,1,0:T(8,128)S(1)} %copy-done.14, bf16[64,32,128]{2,1,0:T(8,128)(2,1)S(1)} %copy-done.27, ...), custom_call_target="tpu_custom_call" | custom-call | flops 201326592 | bytes 10485760 | tf_op jit(solution)/shard_map/between/pallas_call | solution.py:620
  183.9 1.0 copy-done.24
  185.6 1.3 copy-done.3
  187.0 1.1 copy-done.6
  188.0 0.9 copy-done.18
  189.0 11.0 %coupling.3 = (bf16[4,64,32,128]{3,2,1,0:T(8,128)(2,1)}, f32[64,32,128]{2,1,0:T(8,128)S(1)}) custom-call(s32[2]{0:T(128)S(1)} %pad_add_fusion.8.place_ref, s32[48]{0:T(128)S(1)} %compare_select_fusion.14.read_ref.refs_0_, s32[512]{0:T(512)S(1)} %get-tuple-element.129.orbit_ref.refs_1_, s32[48]{0:T(128)S(1)} %compare_select_fusion.13.read_ref.refs_2_, ...), custom_call_target="tpu_custom_call" | custom-call | tf_op jit(solution)/shard_map/coupling/pallas_call | solution.py:549
  200.0 53.8 %all_to_all.20.got_ref = bf16[4,64,32,128]{3,2,1,0:T(8,128)(2,1)} all-to-all(bf16[4,64,32,128]{3,2,1,0:T(8,128)(2,1)} %get-tuple-element.102), channel_id=1, replica_groups=mesh['pairs'=8,'aux'=4] {'aux'}, dimensions={0} | all-to-all | bytes 4194304 | tf_op jit(solution)/shard_map/all_to_all | solution.py:638
  253.8 3.1 %last_update.1 = f32[64,32,128]{2,1,0:T(8,128)} custom-call(s32[2]{0:T(128)S(1)} %pad_add_fusion.8.place_ref, bf16[4,64,32,128]{3,2,1,0:T(8,128)(2,1)} %all_to_all.20.got_ref, f32[64,32,128]{2,1,0:T(8,128)S(1)} %get-tuple-element.103.mine_ref, f32[64,32,128]{2,1,0:T(8,128)S(1)} %copy-done.25, f32[64,32,128]{2,1,0:T(8,128)S(1)} %copy-done.12, ...), custom_call_target="tpu_custom_call" | custom-call | tf_op jit(solution)/shard_map/last_update/pallas_call | solution.py:640
  (181 shorter events, 12.9 us)
Async XLA Ops:
  0.0 16.5 %collective-permute-start.1 = (s32[64,3]{0,1:T(4,128)}, s32[64,3]{0,1:T(4,128)S(1)}, u32[]{:S(2)}, u32[]{:S(2)}) collective-permute-start(s32[64,3]{0,1:T(4,128)} %param.13), channel_id=1, source_target_pairs={{0,3},{1,0},{2,1},{3,2},{4,7},{5,4},{6,5},{7,6},{8,11},{9,8},{10,9... | collective-permute-start | bytes 2312 | tf_op jit(solution)/shard_map/ppermute | solution.py:438
  5.0 11.5 %collective-permute-start.2 = (s32[64,3]{0,1:T(4,128)}, s32[64,3]{0,1:T(4,128)S(1)}, u32[]{:S(2)}, u32[]{:S(2)}) collective-permute-start(s32[64,3]{0,1:T(4,128)} %param.13), channel_id=1, source_target_pairs={{0,1},{1,2},{2,3},{3,0},{4,5},{5,6},{6,7},{7,4},{8,9},{9,10},{10,1... | collective-permute-start | bytes 2312 | tf_op jit(solution)/shard_map/ppermute | solution.py:438
  5.8 10.8 %collective-permute-start = (s32[64,9]{0,1:T(8,128)S(1)}, s32[64,9]{0,1:T(8,128)S(1)}, u32[]{:S(2)}, u32[]{:S(2)}) collective-permute-start(s32[64,9]{0,1:T(8,128)S(1)} %pad_add_fusion), channel_id=1, source_target_pairs={{0,2},{1,3},{2,0},{3,1},{4,6},{5,7},{6,4},{7,5},{8,10},{9,11},{10,... | collective-permute-start | bytes 6920 | tf_op jit(solution)/shard_map/ppermute | solution.py:438
  8.3 7.5 %copy-start.48 = (s32[64,3]{0,1:T(4,128)S(1)}, s32[64,3]{0,1:T(4,128)}, u32[]{:S(2)}) copy-start(s32[64,3]{0,1:T(4,128)} %param.13) | copy-start | bytes 2308
  8.3 10.1 %copy-start.23 = (f32[64,32,128]{2,1,0:T(8,128)S(1)}, f32[64,32,128]{2,1,0:T(8,128)}, u32[]{:S(2)}) copy-start(f32[64,32,128]{2,1,0:T(8,128)} %amps_ref.1) | copy-start | bytes 3145732
  8.3 10.1 %copy-start.40 = (s32[64]{0:T(128)S(1)}, s32[64]{0:T(128)}, u32[]{:S(2)}) copy-start(s32[64]{0:T(128)} %count_ref.3) | copy-start | bytes 772
  13.2 9.7 %collective-permute-start.3 = (bf16[6,256,128]{2,1,0:T(8,128)(2,1)S(1)}, bf16[6,256,128]{2,1,0:T(8,128)(2,1)S(1)}, u32[]{:S(2)}, u32[]{:S(2)}) collective-permute-start(bf16[6,256,128]{2,1,0:T(8,128)(2,1)S(1)} %get-tuple-element.56), channel_id=1, source_target_pairs={{0,8},{4,12},{8,0},{12,4},{16,24},{20,28},{24,16},{28,20},{1,9},{5... | collective-permute-start | bytes 1179656 | tf_op jit(solution)/shard_map/ppermute | solution.py:426
  14.9 10.4 %collective-permute-start.4 = (bf16[6,256,128]{2,1,0:T(8,128)(2,1)S(1)}, bf16[6,256,128]{2,1,0:T(8,128)(2,1)S(1)}, u32[]{:S(2)}, u32[]{:S(2)}) collective-permute-start(bf16[6,256,128]{2,1,0:T(8,128)(2,1)S(1)} %get-tuple-element.57), channel_id=1, source_target_pairs={{0,16},{4,20},{8,24},{12,28},{16,0},{20,4},{24,8},{28,12},{1,17},{... | collective-permute-start | bytes 1179656 | tf_op jit(solution)/shard_map/ppermute | solution.py:426
  18.1 7.2 %copy-start.46 = (s32[8,12,2]{1,0,2:T(8,128)}, s32[8,12,2]{1,0,2:T(8,128)S(1)}, u32[]{:S(2)}) copy-start(s32[8,12,2]{1,0,2:T(8,128)S(1)} %pad_add_fusion.1) | copy-start | bytes 2308
  18.2 17.8 %copy-start.51 = (s32[64,3]{0,1:T(4,128)S(1)}, s32[64,3]{0,1:T(4,128)}, u32[]{:S(2)}) copy-start(s32[64,3]{0,1:T(4,128)} %param.15) | copy-start | bytes 2308
  18.4 17.8 %copy-start.52 = (s32[64,3]{0,1:T(4,128)S(1)}, s32[64,3]{0,1:T(4,128)}, u32[]{:S(2)}) copy-start(s32[64,3]{0,1:T(4,128)} %param.14) | copy-start | bytes 2308
  18.4 18.0 %copy-start.55 = (s32[64,2]{0,1:T(2,128)S(1)}, s32[64,2]{0,1:T(2,128)}, u32[]{:S(2)}) copy-start(s32[64,2]{0,1:T(2,128)} %param.11) | copy-start | bytes 1540
  21.5 30.7 %copy-start.19 = (bf16[64,32,128]{2,1,0:T(8,128)(2,1)}, bf16[64,32,128]{2,1,0:T(8,128)(2,1)S(1)}, u32[]{:S(2)}) copy-start(bf16[64,32,128]{2,1,0:T(8,128)(2,1)S(1)} %get-tuple-element.67.half_ref.before_ref) | copy-start | bytes 1572868
  23.0 15.7 %copy-start.34 = (bf16[6,256,128]{2,1,0:T(8,128)(2,1)}, bf16[6,256,128]{2,1,0:T(8,128)(2,1)S(1)}, u32[]{:S(2)}) copy-start(bf16[6,256,128]{2,1,0:T(8,128)(2,1)S(1)} %collective-permute-done.3.rest_0_) | copy-start | bytes 1179652
  25.3 13.4 %copy-start.36 = (bf16[6,256,128]{2,1,0:T(8,128)(2,1)}, bf16[6,256,128]{2,1,0:T(8,128)(2,1)S(1)}, u32[]{:S(2)}) copy-start(bf16[6,256,128]{2,1,0:T(8,128)(2,1)S(1)} %collective-permute-done.4.rest_2_) | copy-start | bytes 1179652
  25.3 56.4 %all-to-all-start = ((bf16[32,6,32,128]{3,2,1,0:T(8,128)(2,1)}), bf16[32,6,32,128]{3,2,1,0:T(8,128)(2,1)}, u32[]{:S(2)}, u32[]{:S(2)}) async-start(bf16[32,6,32,128]{3,2,1,0:T(8,128)(2,1)} %bitcast.10), calls=%async_computation | async-start | bytes 3145728 | tf_op jit(solution)/shard_map/all_to_all | solution.py:481
  30.3 49.3 %collective-permute-start.5 = (bf16[6,256,128]{2,1,0:T(8,128)(2,1)}, bf16[6,256,128]{2,1,0:T(8,128)(2,1)}, u32[]{:S(2)}, u32[]{:S(2)}) collective-permute-start(bf16[6,256,128]{2,1,0:T(8,128)(2,1)} %get-tuple-element.59), channel_id=1, source_target_pairs={{0,12},{4,8},{8,4},{12,0},{16,28},{20,24},{24,20},{28,16},{1,13},{... | collective-permute-start | bytes 1179656 | tf_op jit(solution)/shard_map/ppermute | solution.py:426
  31.8 47.8 %collective-permute-start.6 = (bf16[6,256,128]{2,1,0:T(8,128)(2,1)}, bf16[6,256,128]{2,1,0:T(8,128)(2,1)}, u32[]{:S(2)}, u32[]{:S(2)}) collective-permute-start(bf16[6,256,128]{2,1,0:T(8,128)(2,1)} %get-tuple-element.61), channel_id=1, source_target_pairs={{0,20},{4,16},{8,28},{12,24},{16,4},{20,0},{24,12},{28,8},{1,21},{... | collective-permute-start | bytes 1179656 | tf_op jit(solution)/shard_map/ppermute | solution.py:426
  33.3 35.5 %collective-permute-start.7 = (bf16[6,256,128]{2,1,0:T(8,128)(2,1)}, bf16[6,256,128]{2,1,0:T(8,128)(2,1)}, u32[]{:S(2)}, u32[]{:S(2)}) collective-permute-start(bf16[6,256,128]{2,1,0:T(8,128)(2,1)} %get-tuple-element.62), channel_id=1, source_target_pairs={{0,4},{4,0},{8,12},{12,8},{16,20},{20,16},{24,28},{28,24},{1,5},{5... | collective-permute-start | bytes 1179656 | tf_op jit(solution)/shard_map/ppermute | solution.py:426
  33.4 36.0 %collective-permute-start.8 = (bf16[6,256,128]{2,1,0:T(8,128)(2,1)}, bf16[6,256,128]{2,1,0:T(8,128)(2,1)}, u32[]{:S(2)}, u32[]{:S(2)}) collective-permute-start(bf16[6,256,128]{2,1,0:T(8,128)(2,1)} %get-tuple-element.63), channel_id=1, source_target_pairs={{0,24},{4,28},{8,16},{12,20},{16,8},{20,12},{24,0},{28,4},{1,25},{... | collective-permute-start | bytes 1179656 | tf_op jit(solution)/shard_map/ppermute | solution.py:426
  33.8 43.1 %collective-permute-start.9 = (bf16[6,256,128]{2,1,0:T(8,128)(2,1)}, bf16[6,256,128]{2,1,0:T(8,128)(2,1)}, u32[]{:S(2)}, u32[]{:S(2)}) collective-permute-start(bf16[6,256,128]{2,1,0:T(8,128)(2,1)} %get-tuple-element.64), channel_id=1, source_target_pairs={{0,28},{4,24},{8,20},{12,16},{16,12},{20,8},{24,4},{28,0},{1,29},{... | collective-permute-start | bytes 1179656 | tf_op jit(solution)/shard_map/ppermute | solution.py:426
  38.7 6.2 %copy-start.54 = (s32[64,3]{0,1:T(4,128)S(1)}, s32[64,3]{0,1:T(4,128)}, u32[]{:S(2)}) copy-start(s32[64,3]{0,1:T(4,128)} %get-tuple-element.122) | copy-start | bytes 2308
  38.7 13.5 %copy-start.16 = (f32[256,256]{1,0:T(8,128)S(1)}, f32[256,256]{1,0:T(8,128)}, u32[]{:S(2)}) copy-start(f32[256,256]{1,0:T(8,128)} %refs_4_.1) | copy-start | bytes 786436
  47.9 2.2 copy-start.49
  52.2 1.6 copy-start.1
  53.8 1.2 copy-start.8
  55.7 12.4 %copy-start.56 = (s32[48]{0:T(128)S(1)}, s32[48]{0:T(128)}, u32[]{:S(2)}) copy-start(s32[48]{0:T(128)} %reshape.216) | copy-start | bytes 580
  68.1 10.6 %copy-start.10 = (f32[64,32,128]{2,1,0:T(8,128)}, f32[64,32,128]{2,1,0:T(8,128)S(1)}, u32[]{:S(2)}) copy-start(f32[64,32,128]{2,1,0:T(8,128)S(1)} %get-tuple-element.96.scale_ref) | copy-start | bytes 3145732
  68.1 10.7 %copy-start.21 = (f32[64,32,128]{2,1,0:T(8,128)}, f32[64,32,128]{2,1,0:T(8,128)S(1)}, u32[]{:S(2)}) copy-start(f32[64,32,128]{2,1,0:T(8,128)S(1)} %get-tuple-element.95.own_ref) | copy-start | bytes 3145732
  68.1 10.7 %copy-start.38 = (f32[64,1,128]{2,1,0:T(1,128)}, f32[64,1,128]{2,1,0:T(1,128)S(1)}, u32[]{:S(2)}) copy-start(f32[64,1,128]{2,1,0:T(1,128)S(1)} %get-tuple-element.98.energy_ref) | copy-start | bytes 98308
  68.8 10.8 %copy-start.35 = (bf16[6,256,128]{2,1,0:T(8,128)(2,1)S(1)}, bf16[6,256,128]{2,1,0:T(8,128)(2,1)}, u32[]{:S(2)}) copy-start(bf16[6,256,128]{2,1,0:T(8,128)(2,1)} %copy-done.34) | copy-start | bytes 1179652
  68.8 10.8 %copy-start.37 = (bf16[6,256,128]{2,1,0:T(8,128)(2,1)S(1)}, bf16[6,256,128]{2,1,0:T(8,128)(2,1)}, u32[]{:S(2)}) copy-start(bf16[6,256,128]{2,1,0:T(8,128)(2,1)} %copy-done.36) | copy-start | bytes 1179652
  96.5 4.6 %copy-start.47 = (s32[8,12,2]{1,0,2:T(8,128)S(1)}, s32[8,12,2]{1,0,2:T(8,128)}, u32[]{:S(2)}) copy-start(s32[8,12,2]{1,0,2:T(8,128)} %copy-done.46) | copy-start | bytes 2308
  96.5 4.7 %copy-start.42 = (s32[48]{0:T(128)S(1)}, s32[48]{0:T(128)}, u32[]{:S(2)}) copy-start(s32[48]{0:T(128)} %compare_select_fusion.7.send_ref) | copy-start | bytes 580
  96.5 54.5 %all-to-all-start.1 = ((f16[4,65,32,128]{3,2,1,0:T(8,128)(2,1)}), f16[4,65,32,128]{3,2,1,0:T(8,128)(2,1)}, u32[]{:S(2)}, u32[]{:S(2)}) async-start(f16[4,65,32,128]{3,2,1,0:T(8,128)(2,1)} %multiply_convert_fusion), calls=%async_computation.1 | async-start | bytes 4259840 | tf_op jit(solution)/shard_map/all_to_all | solution.py:585
  105.5 2.1 copy-start.43
  105.5 2.8 %copy-start.44 = (bf16[6,256,128]{2,1,0:T(8,128)(2,1)}, bf16[6,256,128]{2,1,0:T(8,128)(2,1)S(1)}, u32[]{:S(2)}) copy-start(bf16[6,256,128]{2,1,0:T(8,128)(2,1)S(1)} %get-tuple-element.85) | copy-start | bytes 1179652
  105.5 4.2 %copy-start.45 = (bf16[6,256,128]{2,1,0:T(8,128)(2,1)}, bf16[6,256,128]{2,1,0:T(8,128)(2,1)S(1)}, u32[]{:S(2)}) copy-start(bf16[6,256,128]{2,1,0:T(8,128)(2,1)S(1)} %get-tuple-element.80) | copy-start | bytes 1179652
  105.5 11.9 %collective-permute-start.10 = (bf16[6,256,128]{2,1,0:T(8,128)(2,1)}, bf16[6,256,128]{2,1,0:T(8,128)(2,1)S(1)}, u32[]{:S(2)}, u32[]{:S(2)}) collective-permute-start(bf16[6,256,128]{2,1,0:T(8,128)(2,1)} %get-tuple-element.76), channel_id=1, source_target_pairs={{0,8},{4,12},{8,0},{12,4},{16,24},{20,28},{24,16},{28,20},{1,9},{5... | collective-permute-start | bytes 1179656 | tf_op jit(solution)/shard_map/ppermute | solution.py:574
  107.5 18.7 %collective-permute-start.11 = (bf16[6,256,128]{2,1,0:T(8,128)(2,1)}, bf16[6,256,128]{2,1,0:T(8,128)(2,1)S(1)}, u32[]{:S(2)}, u32[]{:S(2)}) collective-permute-start(bf16[6,256,128]{2,1,0:T(8,128)(2,1)} %get-tuple-element.77), channel_id=1, source_target_pairs={{0,12},{4,8},{8,4},{12,0},{16,28},{20,24},{24,20},{28,16},{1,13},{... | collective-permute-start | bytes 1179656 | tf_op jit(solution)/shard_map/ppermute | solution.py:574
  108.3 18.6 %collective-permute-start.12 = (bf16[6,256,128]{2,1,0:T(8,128)(2,1)}, bf16[6,256,128]{2,1,0:T(8,128)(2,1)S(1)}, u32[]{:S(2)}, u32[]{:S(2)}) collective-permute-start(bf16[6,256,128]{2,1,0:T(8,128)(2,1)} %get-tuple-element.78), channel_id=1, source_target_pairs={{0,16},{4,20},{8,24},{12,28},{16,0},{20,4},{24,8},{28,12},{1,17},{... | collective-permute-start | bytes 1179656 | tf_op jit(solution)/shard_map/ppermute | solution.py:574
  108.5 19.2 %collective-permute-start.13 = (bf16[6,256,128]{2,1,0:T(8,128)(2,1)}, bf16[6,256,128]{2,1,0:T(8,128)(2,1)}, u32[]{:S(2)}, u32[]{:S(2)}) collective-permute-start(bf16[6,256,128]{2,1,0:T(8,128)(2,1)} %get-tuple-element.79), channel_id=1, source_target_pairs={{0,20},{4,16},{8,28},{12,24},{16,4},{20,0},{24,12},{28,8},{1,21},{... | collective-permute-start | bytes 1179656 | tf_op jit(solution)/shard_map/ppermute | solution.py:574
  109.7 44.4 %copy-start.9 = (f32[64,32,128]{2,1,0:T(8,128)S(1)}, f32[64,32,128]{2,1,0:T(8,128)}, u32[]{:S(2)}) copy-start(f32[64,32,128]{2,1,0:T(8,128)} %copy-done.7) | copy-start | bytes 3145732
  117.4 36.7 %copy-start.28 = (bf16[6,256,128]{2,1,0:T(8,128)(2,1)}, bf16[6,256,128]{2,1,0:T(8,128)(2,1)S(1)}, u32[]{:S(2)}) copy-start(bf16[6,256,128]{2,1,0:T(8,128)(2,1)S(1)} %collective-permute-done.10.rest_1_) | copy-start | bytes 1179652
  127.7 26.4 %collective-permute-start.14 = (bf16[6,256,128]{2,1,0:T(8,128)(2,1)}, bf16[6,256,128]{2,1,0:T(8,128)(2,1)}, u32[]{:S(2)}, u32[]{:S(2)}) collective-permute-start(bf16[6,256,128]{2,1,0:T(8,128)(2,1)} %copy-done.45), channel_id=1, source_target_pairs={{0,4},{4,0},{8,12},{12,8},{16,20},{20,16},{24,28},{28,24},{1,5},{5... | collective-permute-start | bytes 1179656 | tf_op jit(solution)/shard_map/ppermute | solution.py:574
  127.9 26.2 %collective-permute-start.15 = (bf16[6,256,128]{2,1,0:T(8,128)(2,1)}, bf16[6,256,128]{2,1,0:T(8,128)(2,1)}, u32[]{:S(2)}, u32[]{:S(2)}) collective-permute-start(bf16[6,256,128]{2,1,0:T(8,128)(2,1)} %copy-done.44), channel_id=1, source_target_pairs={{0,24},{4,28},{8,16},{12,20},{16,8},{20,12},{24,0},{28,4},{1,25},{... | collective-permute-start | bytes 1179656 | tf_op jit(solution)/shard_map/ppermute | solution.py:574
  129.8 24.3 %collective-permute-start.16 = (bf16[6,256,128]{2,1,0:T(8,128)(2,1)}, bf16[6,256,128]{2,1,0:T(8,128)(2,1)}, u32[]{:S(2)}, u32[]{:S(2)}) collective-permute-start(bf16[6,256,128]{2,1,0:T(8,128)(2,1)} %copy-done.43), channel_id=1, source_target_pairs={{0,28},{4,24},{8,20},{12,16},{16,12},{20,8},{24,4},{28,0},{1,29},{... | collective-permute-start | bytes 1179656 | tf_op jit(solution)/shard_map/ppermute | solution.py:574
  154.1 1.2 copy-start.11
  155.4 1.2 copy-start.22
  160.6 3.9 %copy-start.50 = (s32[8,3]{0,1:T(4,128)S(1)}, s32[8,3]{0,1:T(4,128)}, u32[]{:S(2)}) copy-start(s32[8,3]{0,1:T(4,128)} %copy-done.49) | copy-start | bytes 292
  160.6 3.9 %copy-start.53 = (s32[8,3]{0,1:T(4,128)S(1)}, s32[8,3]{0,1:T(4,128)}, u32[]{:S(2)}) copy-start(s32[8,3]{0,1:T(4,128)} %get-tuple-element.106) | copy-start | bytes 292
  160.6 25.0 %all-to-all-start.2 = ((bf16[16,12,32,128]{3,2,1,0:T(8,128)(2,1)}), bf16[16,12,32,128]{3,2,1,0:T(8,128)(2,1)S(1)}, u32[]{:S(2)}, u32[]{:S(2)}) async-start(bf16[16,12,32,128]{3,2,1,0:T(8,128)(2,1)} %bitcast.67), calls=%async_computation.2 | async-start | bytes 3145728 | tf_op jit(solution)/shard_map/all_to_all | solution.py:616
  164.7 4.9 %copy-start.29 = (bf16[6,256,128]{2,1,0:T(8,128)(2,1)S(1)}, bf16[6,256,128]{2,1,0:T(8,128)(2,1)}, u32[]{:S(2)}) copy-start(bf16[6,256,128]{2,1,0:T(8,128)(2,1)} %copy-done.28) | copy-start | bytes 1179652
  164.7 4.9 %copy-start.31 = (bf16[6,256,128]{2,1,0:T(8,128)(2,1)S(1)}, bf16[6,256,128]{2,1,0:T(8,128)(2,1)}, u32[]{:S(2)}) copy-start(bf16[6,256,128]{2,1,0:T(8,128)(2,1)} %copy-done.30) | copy-start | bytes 1179652
  164.7 4.9 %copy-start.33 = (bf16[6,256,128]{2,1,0:T(8,128)(2,1)S(1)}, bf16[6,256,128]{2,1,0:T(8,128)(2,1)}, u32[]{:S(2)}) copy-start(bf16[6,256,128]{2,1,0:T(8,128)(2,1)} %copy-done.32) | copy-start | bytes 1179652
  168.1 1.5 copy-start
  169.6 5.1 %copy-start.14 = (f32[64,32,128]{2,1,0:T(8,128)S(1)}, f32[64,32,128]{2,1,0:T(8,128)}, u32[]{:S(2)}) copy-start(f32[64,32,128]{2,1,0:T(8,128)} %copy-done.13) | copy-start | bytes 3145732
  169.6 5.1 %copy-start.20 = (bf16[64,32,128]{2,1,0:T(8,128)(2,1)S(1)}, bf16[64,32,128]{2,1,0:T(8,128)(2,1)}, u32[]{:S(2)}) copy-start(bf16[64,32,128]{2,1,0:T(8,128)(2,1)} %copy-done.19) | copy-start | bytes 1572868
  169.7 5.1 %copy-start.27 = (bf16[64,32,128]{2,1,0:T(8,128)(2,1)S(1)}, bf16[64,32,128]{2,1,0:T(8,128)(2,1)}, u32[]{:S(2)}) copy-start(bf16[64,32,128]{2,1,0:T(8,128)(2,1)} %copy-done.26) | copy-start | bytes 1572868
  169.7 5.1 %copy-start.39 = (f32[64,1,128]{2,1,0:T(1,128)S(1)}, f32[64,1,128]{2,1,0:T(1,128)}, u32[]{:S(2)}) copy-start(f32[64,1,128]{2,1,0:T(1,128)} %copy-done.38) | copy-start | bytes 98308
  185.6 1.3 copy-start.3
  200.0 53.8 %copy-start.12 = (f32[64,32,128]{2,1,0:T(8,128)S(1)}, f32[64,32,128]{2,1,0:T(8,128)}, u32[]{:S(2)}) copy-start(f32[64,32,128]{2,1,0:T(8,128)} %copy-done.10) | copy-start | bytes 3145732
  200.0 53.8 %copy-start.15 = (f32[64,32,128]{2,1,0:T(8,128)S(1)}, f32[64,32,128]{2,1,0:T(8,128)}, u32[]{:S(2)}) copy-start(f32[64,32,128]{2,1,0:T(8,128)} %copy-done.13) | copy-start | bytes 3145732
  200.0 53.8 %copy-start.25 = (f32[64,32,128]{2,1,0:T(8,128)S(1)}, f32[64,32,128]{2,1,0:T(8,128)}, u32[]{:S(2)}) copy-start(f32[64,32,128]{2,1,0:T(8,128)} %copy-done.24) | copy-start | bytes 3145732
  (13 other events, 11.8 us)
